TPU v7x, 32 devices: a whole 2x2x4 slice. The times are simulated.
32 devices in a mesh: dp: 8 (over z, y), pipe: 4 (over x, core).
Axes of the slice: x: 2, y: 2, z: 4, core: 2. Of those that a mesh axis runs over, the one named last changes fastest.
Arguments:
- teach_in: bfloat16 [4, 16, 12, 12, 1024], P('pipe', 'dp'), may hold values from -6 to 6
- stud_in: bfloat16 [4, 24, 8, 8, 1024], P('pipe', 'dp'), may hold values from -6 to 6
- params: float32 [4, 4986880], P('pipe', 'dp')
- owners: int32 [4, 8], P('pipe'), may hold values from 0 to 7, as said below
- depth_gates: int32 [4], replicated, may hold values from 0 to 1, as said below
- teach_ids: int32 [4, 16], P(None, 'dp'), may hold values from 0 to 31, as said below
- stud_ids: int32 [4, 24], P(None, 'dp'), may hold values from 0 to 31, as said below
- targets: float32 [32, 2048], replicated, may hold values from -6 to 6
- moment: float32 [4, 4986880], P('pipe', 'dp'), may hold values from -0.00048828125 to 0.00048828125
- second: float32 [4, 4986880], P('pipe', 'dp'), may hold values from 2.475685e-09 to 1.9995918e-08
- gram_stats: float32 [4, 1024, 128], P('pipe', 'dp')
- eigen_basis: float32 [4, 1024, 128], P('pipe', 'dp')
Outputs:
- segment_teach: bfloat16 [4, 4, 16, 6, 6, 2048], P('pipe', None, 'dp')
- segment_stud: bfloat16 [4, 4, 24, 4, 4, 2048], P('pipe', None, 'dp')
- grad_teach: bfloat16 [4, 16, 12, 12, 1024], P('pipe', 'dp')
- grad_stud: bfloat16 [4, 24, 8, 8, 1024], P('pipe', 'dp')
- norm_stats: float32 [4, 4, 8, 2, 3072], P('pipe', None, 'dp')
- grad_norm: float32 [], replicated
- clipped_grads: float32 [4, 4986880], P('pipe', 'dp')
- moment_new: float32 [4, 4986880], P('pipe', 'dp')
- second_new: float32 [4, 4986880], P('pipe', 'dp')
- params_new: float32 [4, 4986880], P('pipe', 'dp')
- gram_new: float32 [4, 1024, 128], P('pipe', 'dp')
- basis_new: float32 [4, 1024, 128], P('pipe', 'dp')
Inputs may be any that keep to these rules, and one draw needn't show every extreme that they name: `owners`: each row is a permutation. `depth_gates`: exactly one micro-batch has gate 0. `teach_ids`: every image has exactly two teacher crops. `stud_ids`: every image has exactly three student crops.
All inputs are finite; a program needn't handle non-finite values.
Results may differ from a plain program's by a relative error of at most 0.02.
Values may be sent and summed in bfloat16 or wider, within the bound.
A program may use at most 896 MiB of HBM per device.

v0:
```python
import functools
import math

import jax
import jax.numpy as jnp
import numpy as np
from jax import lax
from jax.experimental import pallas as pl
from jax.experimental.pallas import tpu as pltpu
from jax.sharding import PartitionSpec as P

C_IN = 1024
MID = 512
C_OUT = 2048
STEP = 10
NS_STEPS = 5


HIGH = lax.Precision.HIGHEST
NORM_EPS = 1e-05
POOL_EPS = 1e-06
CLIP_NORM = 1.0
LEARN_RATE = 0.02
DECAY_FIRST = 0.9
DECAY_SECOND = 0.95
DECAY_STATS = 0.95
ADAM_EPS = 1e-08
WEIGHT_DECAY = 0.01


def section_shapes(section):
    if section == 0:
        return [
            ("first_conv", (C_IN, MID)),
            ("middle_conv", (9 * MID, MID)),
            ("skip_conv", (C_IN, C_OUT)),
            ("first_gain", (MID,)),
            ("first_bias", (MID,)),
            ("middle_gain", (MID,)),
            ("middle_bias", (MID,)),
            ("skip_gain", (C_OUT,)),
            ("skip_bias", (C_OUT,)),
        ]
    if section == 2:
        return [
            ("first_conv", (C_OUT, MID)),
            ("middle_conv", (9 * MID, MID)),
            ("first_gain", (MID,)),
            ("first_bias", (MID,)),
            ("middle_gain", (MID,)),
            ("middle_bias", (MID,)),
        ]
    return [("last_conv", (MID, C_OUT)), ("last_gain", (C_OUT,)), ("last_bias", (C_OUT,))]


def unpack(flat_vector, section):
    pieces = {}
    offset = 0
    for entry_name, entry_shape in section_shapes(section):
        entry_size = math.prod(entry_shape)
        pieces[entry_name] = flat_vector[offset : offset + entry_size].reshape(entry_shape)
        offset = offset + entry_size
    return pieces


def pack(grads, section, flat_size):
    parts = [grads[entry_name].reshape(-1) for entry_name, entry_shape in section_shapes(section)]
    used = sum((math.prod(entry_shape) for entry_name, entry_shape in section_shapes(section)))
    parts.append(jnp.zeros((flat_size - used,), jnp.float32))
    return jnp.concatenate(parts)


def as_float(vector):
    return vector.astype(jnp.float32)


def to_low(groups):
    return tuple((portion.astype(jnp.bfloat16) for portion in groups))


def to_high(groups):
    return tuple((portion.astype(jnp.float32) for portion in groups))


def point_conv(groups, weight):
    return tuple(
        (
            jnp.einsum("khwc,cd->khwd", portion, weight, preferred_element_type=jnp.float32)
            for portion in groups
        )
    )


def point_back(grad_out, groups, weight):
    low_grads = to_low(grad_out)
    grad_input = tuple(
        (
            jnp.einsum("khwd,cd->khwc", grad_part, weight, preferred_element_type=jnp.float32)
            for grad_part in low_grads
        )
    )
    grad_weight = sum(
        (
            jnp.einsum("khwc,khwd->cd", in_part, grad_part, preferred_element_type=jnp.float32)
            for in_part, grad_part in zip(groups, low_grads)
        )
    )
    return (grad_input, grad_weight)


def patches(portion, stride):
    height = portion.shape[1]
    across = portion.shape[2]
    padded = jnp.pad(portion, ((0, 0), (1, 1), (1, 1), (0, 0)))
    shifted = [
        padded[:, row_off : row_off + height : stride, col_off : col_off + across : stride, :]
        for row_off in range(3)
        for col_off in range(3)
    ]
    return jnp.concatenate(shifted, axis=-1)


def area_conv(groups, weight, stride):
    columns = tuple((patches(portion, stride) for portion in groups))
    return (point_conv(columns, weight), columns)


def unpatch(grad_cols, height, across, stride):
    channels = grad_cols.shape[-1] // 9
    padded = jnp.zeros((grad_cols.shape[0], height + 2, across + 2, channels), jnp.float32)
    for row_off in range(3):
        for col_off in range(3):
            offset = (3 * row_off + col_off) * channels
            padded = padded.at[
                :, row_off : row_off + height : stride, col_off : col_off + across : stride, :
            ].add(grad_cols[..., offset : offset + channels])
    return padded[:, 1 : height + 1, 1 : across + 1, :]


def area_back(grad_out, columns, weight, stride, in_shapes):
    grad_cols, grad_weight = point_back(grad_out, columns, weight)
    grad_input = tuple(
        (
            unpatch(grad_part, shape_item[1], shape_item[2], stride)
            for grad_part, shape_item in zip(grad_cols, in_shapes)
        )
    )
    return (grad_input, grad_weight)


def batch_norm(groups, gain, bias):
    rows_total = sum((portion.shape[0] * portion.shape[1] * portion.shape[2] for portion in groups))
    centre = sum((jnp.sum(portion, axis=(0, 1, 2)) for portion in groups)) / rows_total
    spread = (
        sum((jnp.sum(jnp.square(portion - centre), axis=(0, 1, 2)) for portion in groups))
        / rows_total
    )
    inverse = lax.rsqrt(spread + NORM_EPS)
    standard = tuple(((portion - centre) * inverse for portion in groups))
    normed = tuple((gain * std_part + bias for std_part in standard))
    return (normed, (centre, spread, inverse, standard))


def norm_back(grad_out, gain, saved):
    centre, spread, inverse, standard = saved
    rows_total = sum(
        (portion.shape[0] * portion.shape[1] * portion.shape[2] for portion in standard)
    )
    grad_sum = sum((jnp.sum(grad_part, axis=(0, 1, 2)) for grad_part in grad_out))
    grad_dot = sum(
        (
            jnp.sum(grad_part * std_part, axis=(0, 1, 2))
            for grad_part, std_part in zip(grad_out, standard)
        )
    )
    grad_input = tuple(
        (
            gain
            * inverse
            * (grad_part - grad_sum / rows_total - std_part * (grad_dot / rows_total))
            for grad_part, std_part in zip(grad_out, standard)
        )
    )
    return (grad_input, grad_dot, grad_sum)


def through_softplus(grad_out, pre_values):
    return tuple(
        (grad_part * jax.nn.sigmoid(pre_part) for grad_part, pre_part in zip(grad_out, pre_values))
    )


def front_forward(pieces, inputs):
    first = point_conv(inputs, pieces["first_conv"])
    normed_a, saved_a = batch_norm(
        first, as_float(pieces["first_gain"]), as_float(pieces["first_bias"])
    )
    hidden = tuple((jax.nn.softplus(portion).astype(jnp.bfloat16) for portion in normed_a))
    middle, columns = area_conv(hidden, pieces["middle_conv"], 2)
    normed_b, saved_b = batch_norm(
        middle, as_float(pieces["middle_gain"]), as_float(pieces["middle_bias"])
    )
    narrow = tuple((jax.nn.softplus(portion) for portion in normed_b))
    reduced = tuple((portion[:, ::2, ::2, :] for portion in inputs))
    skipped = point_conv(reduced, pieces["skip_conv"])
    wide, saved_p = batch_norm(
        skipped, as_float(pieces["skip_gain"]), as_float(pieces["skip_bias"])
    )
    norm_rows = jnp.stack(
        [
            jnp.concatenate([saved_a[0], saved_b[0], saved_p[0]]),
            jnp.concatenate([saved_a[1], saved_b[1], saved_p[1]]),
        ]
    )
    kept = (normed_a, hidden, columns, normed_b, reduced, saved_a, saved_b, saved_p)
    return (wide, narrow, norm_rows, kept)


def front_backward(pieces, inputs, grad_wide, grad_narrow):
    wide, narrow, norm_rows, kept = front_forward(pieces, inputs)
    normed_a, hidden, columns, normed_b, reduced, saved_a, saved_b, saved_p = kept
    grads = {}
    grad_pre_b = through_softplus(grad_narrow, normed_b)
    grad_mid, grads["middle_gain"], grads["middle_bias"] = norm_back(
        grad_pre_b, as_float(pieces["middle_gain"]), saved_b
    )
    grad_hidden, grads["middle_conv"] = area_back(
        grad_mid, columns, pieces["middle_conv"], 2, [portion.shape for portion in hidden]
    )
    grad_pre_a = through_softplus(grad_hidden, normed_a)
    grad_first, grads["first_gain"], grads["first_bias"] = norm_back(
        grad_pre_a, as_float(pieces["first_gain"]), saved_a
    )
    grad_inputs, grads["first_conv"] = point_back(grad_first, inputs, pieces["first_conv"])
    grad_skip, grads["skip_gain"], grads["skip_bias"] = norm_back(
        grad_wide, as_float(pieces["skip_gain"]), saved_p
    )
    grad_reduced, grads["skip_conv"] = point_back(grad_skip, reduced, pieces["skip_conv"])
    grad_inputs = tuple(
        (
            full_part.at[:, ::2, ::2, :].add(part_reduced)
            for full_part, part_reduced in zip(grad_inputs, grad_reduced)
        )
    )
    return (grad_inputs, grads)


def join_forward(pieces, wide, narrow):
    last = point_conv(narrow, pieces["last_conv"])
    normed, saved = batch_norm(last, as_float(pieces["last_gain"]), as_float(pieces["last_bias"]))
    pre_values = tuple(
        (
            skip_part.astype(jnp.float32) + branch_part
            for skip_part, branch_part in zip(wide, normed)
        )
    )
    ending = tuple((jax.nn.softplus(pre_part) for pre_part in pre_values))
    filler = jnp.zeros((2 * MID,), jnp.float32)
    norm_rows = jnp.stack(
        [jnp.concatenate([saved[0], filler]), jnp.concatenate([saved[1], filler])]
    )
    return (ending, norm_rows, (pre_values, saved))


def join_grads(pieces, narrow, kept, grad_out, gate):
    pre_values, saved = kept
    grad_pre = tuple(
        (
            grad_part * jax.nn.sigmoid(pre_part) * gate
            for grad_part, pre_part in zip(grad_out, pre_values)
        )
    )
    grad_wide = tuple(
        (pre_grad + grad_part * (1.0 - gate) for pre_grad, grad_part in zip(grad_pre, grad_out))
    )
    grad_last, gain_grad, bias_grad = norm_back(grad_pre, as_float(pieces["last_gain"]), saved)
    grad_narrow, weight_grad = point_back(grad_last, narrow, pieces["last_conv"])
    grads = {"last_conv": weight_grad, "last_gain": gain_grad, "last_bias": bias_grad}
    return (grad_wide, grad_narrow, grads)


def split_forward(pieces, wide):
    first = point_conv(wide, pieces["first_conv"])
    normed_a, saved_a = batch_norm(
        first, as_float(pieces["first_gain"]), as_float(pieces["first_bias"])
    )
    hidden = tuple((jax.nn.softplus(portion).astype(jnp.bfloat16) for portion in normed_a))
    middle, columns = area_conv(hidden, pieces["middle_conv"], 1)
    normed_b, saved_b = batch_norm(
        middle, as_float(pieces["middle_gain"]), as_float(pieces["middle_bias"])
    )
    narrow = tuple((jax.nn.softplus(portion) for portion in normed_b))
    filler = jnp.zeros((C_OUT,), jnp.float32)
    norm_rows = jnp.stack(
        [
            jnp.concatenate([saved_a[0], saved_b[0], filler]),
            jnp.concatenate([saved_a[1], saved_b[1], filler]),
        ]
    )
    return (narrow, norm_rows, (normed_a, hidden, columns, normed_b, saved_a, saved_b))


def split_backward(pieces, wide, grad_relay, grad_narrow):
    narrow, norm_rows, kept = split_forward(pieces, wide)
    normed_a, hidden, columns, normed_b, saved_a, saved_b = kept
    grads = {}
    grad_pre_b = through_softplus(grad_narrow, normed_b)
    grad_mid, grads["middle_gain"], grads["middle_bias"] = norm_back(
        grad_pre_b, as_float(pieces["middle_gain"]), saved_b
    )
    grad_hidden, grads["middle_conv"] = area_back(
        grad_mid, columns, pieces["middle_conv"], 1, [portion.shape for portion in hidden]
    )
    grad_pre_a = through_softplus(grad_hidden, normed_a)
    grad_first, grads["first_gain"], grads["first_bias"] = norm_back(
        grad_pre_a, as_float(pieces["first_gain"]), saved_a
    )
    grad_conv_in, grads["first_conv"] = point_back(grad_first, wide, pieces["first_conv"])
    grad_wide = tuple(
        (relay_part + conv_part for relay_part, conv_part in zip(grad_relay, grad_conv_in))
    )
    return (grad_wide, grads)


def pool_grad(final, targets, picks):
    result = []
    for portion, pick_ids in zip(final, picks):
        cubes = jnp.mean(portion * portion * portion, axis=(1, 2)) + POOL_EPS
        factor = jnp.exp(jnp.log(cubes) * (-2.0 / 3.0)) * targets[pick_ids]
        result.append(factor[:, None, None, :] * portion * portion)
    return tuple(result)


def used_size(section):
    return sum((math.prod(entry_shape) for entry_name, entry_shape in section_shapes(section)))


def batch_pass(reals, inputs, gate, targets, picks):
    pieces = [unpack(reals[section], section) for section in range(4)]
    wide_f, narrow_f, rows_0, _ = front_forward(pieces[0], inputs)
    wide_0, narrow_0 = to_low(wide_f), to_low(narrow_f)
    ending_1, rows_1, kept_1 = join_forward(pieces[1], wide_0, narrow_0)
    wide_1 = to_low(ending_1)
    narrow_f, rows_2, _ = split_forward(pieces[2], wide_1)
    narrow_2 = to_low(narrow_f)
    ending_3, rows_3, kept_3 = join_forward(pieces[3], wide_1, narrow_2)
    final = tuple(
        (
            jnp.where(gate > 0, end_part, relay_part.astype(jnp.float32))
            for end_part, relay_part in zip(ending_3, wide_1)
        )
    )
    cotangent = pool_grad(final, targets, picks)
    grad_wide, grad_narrow, grads_3 = join_grads(pieces[3], narrow_2, kept_3, cotangent, gate)
    grad_wide, grads_2 = split_backward(
        pieces[2], wide_1, to_high(to_low(grad_wide)), to_high(to_low(grad_narrow))
    )
    grad_wide, grad_narrow, grads_1 = join_grads(
        pieces[1], narrow_0, kept_1, to_high(to_low(grad_wide)), 1.0
    )
    grad_inputs, grads_0 = front_backward(
        pieces[0], inputs, to_high(to_low(grad_wide)), to_high(to_low(grad_narrow))
    )
    outs = (wide_0, wide_1, wide_1, to_low(final))
    stats = jnp.stack([rows_0, rows_1, rows_2 * gate, rows_3 * gate])
    return (outs, stats, to_low(grad_inputs), (grads_0, grads_1, grads_2, grads_3))


def on_device(
    teach_in,
    stud_in,
    params,
    owners,
    depth_gates,
    teach_ids,
    stud_ids,
    targets,
    moment,
    second,
    gram_stats,
    eigen_basis,
):
    sections = lax.axis_size("pipe")
    rank = lax.axis_index("pipe")
    owner_count = lax.axis_size("dp")
    span_size = params.shape[1]
    flat_size = span_size * owner_count
    owner_rows = lax.all_gather(owners, "pipe", axis=0, tiled=True)
    gathered = lax.all_gather(params[0].astype(jnp.bfloat16), ("pipe", "dp"), axis=0)
    gathered = gathered.reshape(sections, owner_count, span_size)
    reals = []
    for section in range(sections):
        inverse = jnp.argsort(owner_rows[section]).astype(jnp.int32)
        blocks = -(-used_size(section) // span_size)
        reals.append(gathered[section][inverse[:blocks]].reshape(blocks * span_size))
    inputs = (teach_in[0], stud_in[0])
    gate = depth_gates[rank].astype(jnp.float32)
    outs, stats, (teach_grad, stud_grad), grads = batch_pass(
        reals, inputs, gate, targets, (teach_ids[rank], stud_ids[rank])
    )
    segment_teach = lax.all_to_all(
        jnp.stack([part[0] for part in outs]), "pipe", split_axis=0, concat_axis=0, tiled=True
    )
    segment_stud = lax.all_to_all(
        jnp.stack([part[1] for part in outs]), "pipe", split_axis=0, concat_axis=0, tiled=True
    )
    stats = lax.all_to_all(stats, "pipe", split_axis=0, concat_axis=0, tiled=True)
    rows = []
    for section in range(sections):
        flat = pack(grads[section], section, flat_size).reshape(owner_count, span_size)
        rows.append(flat[owner_rows[section]])
    span_total = lax.psum_scatter(
        jnp.stack(rows).reshape(sections * owner_count, span_size),
        ("pipe", "dp"),
        scatter_dimension=0,
        tiled=True,
    ).reshape(span_size)
    total_squares = lax.psum(jnp.sum(span_total * span_total), ("dp", "pipe"))
    grad_norm = jnp.sqrt(total_squares)
    factor = jnp.minimum(1.0, CLIP_NORM / grad_norm)
    clipped = span_total * factor
    matrix = clipped.reshape(span_size // 128, 128)
    gram_old = gram_stats[0]
    basis_old = eigen_basis[0]
    gram_new = DECAY_STATS * gram_old + (1.0 - DECAY_STATS) * jnp.dot(
        matrix.T, matrix, precision=HIGH
    )
    product = jnp.dot(gram_new, basis_old, precision=HIGH)
    rotation = product / jnp.sqrt(jnp.sum(product * product))
    for repeat in range(NS_STEPS):
        square = jnp.dot(rotation.T, rotation, precision=HIGH)
        rotation = 1.5 * rotation - 0.5 * jnp.dot(rotation, square, precision=HIGH)
    moment_old = moment.reshape(span_size // 128, 128)
    initial = jnp.dot(moment_old, basis_old.T, precision=HIGH)
    blended = DECAY_FIRST * initial + (1.0 - DECAY_FIRST) * matrix
    moment_new = jnp.dot(blended, rotation, precision=HIGH)
    rotated = jnp.dot(matrix, rotation, precision=HIGH)
    second_new = (
        DECAY_SECOND * second.reshape(span_size // 128, 128)
        + (1.0 - DECAY_SECOND) * rotated * rotated
    )
    correction = math.sqrt(1.0 - DECAY_SECOND**STEP) / (1.0 - DECAY_FIRST**STEP)
    direction = (
        jnp.dot(moment_new / (jnp.sqrt(second_new) + ADAM_EPS), rotation.T, precision=HIGH)
        * correction
    )
    weights = params.reshape(span_size // 128, 128)
    params_new = weights - LEARN_RATE * (direction + WEIGHT_DECAY * weights)
    return (
        segment_teach[None],
        segment_stud[None],
        teach_grad[None],
        stud_grad[None],
        stats[None, :, None],
        grad_norm,
        clipped.reshape(1, span_size),
        moment_new.reshape(1, span_size),
        second_new.reshape(1, span_size),
        params_new.reshape(1, span_size),
        gram_new[None],
        rotation[None],
    )


MESH = pl.DeviceIdType.MESH
LOW = jnp.bfloat16
FULL = jnp.float32
TILE = 256
WINDOW = 20
STRIDE = 19
EDGE = 64
BIG_ROWS = STRIDE * TILE + EDGE
VEC_TILE = (152, 32, 104, 32)
USED_TILES = (153, 33, 105, 33)
FRONT_WIDE = 88
SMALL_ROWS = 1056
ROWS = 120
PADDED = 128
STUD_ROWS = 48
TEACH_END = 80


def any_spec():
    return pl.BlockSpec(memory_space=pl.ANY)


def smem_spec():
    return pl.BlockSpec(memory_space=pltpu.SMEM)


def vmem_spec():
    return pl.BlockSpec(memory_space=pltpu.VMEM)


def tile_forms(section, tile):
    even = lax.rem(section, 2) == 0
    vector = jnp.where(section == 0, 152, jnp.where(section == 2, 104, 32))
    narrow_end = jnp.where(section == 0, FRONT_WIDE, jnp.where(section == 2, 104, 0))
    narrow = even & (tile < narrow_end)
    plain = tile == vector
    return narrow, plain


def prepare_kernel(owners, params, big, small, ids, flat, sem):
    block, section = owners[0, lax.axis_index("dp")], lax.axis_index("pipe")

    even = lax.rem(section, 2) == 0
    flat[0:EDGE, :] = jnp.zeros((EDGE, 128), FULL)
    flat[STRIDE * TILE : WINDOW * TILE, :] = jnp.zeros((TILE, 128), FULL)
    copy = pltpu.make_async_copy(params.at[:, 0, :], flat.at[pl.ds(6 * block, params.shape[0])], sem)
    copy.start()

    @pl.when(jnp.logical_not(even))
    def _():
        @pl.loop(0, small.shape[0])
        def _(r):
            small[r] = jnp.zeros((TILE, 128), LOW)

    lane = lax.broadcasted_iota(jnp.int32, (8, 128), 1)
    row = jnp.zeros((8, 128), jnp.int32)
    for j in range(8):
        row = jnp.where(lane == j, owners[0, j], row)
    ids[...] = row
    copy.wait()

    def wide_tile(base):
        return [flat[pl.ds(base + j, 16, 16), :].astype(LOW) for j in range(16)]

    @pl.when(even)
    def _():
        @pl.loop(0, STRIDE)
        def _(r):
            narrow, plain = tile_forms(section, STRIDE * block + r)
            base = pl.multiple_of(TILE * r, TILE)

            @pl.when(narrow)
            def _():
                for j in range(4):
                    big[pl.ds(base + 64 * j, 64), :] = flat[pl.ds(base + j, 64, 4), :].astype(LOW)

            @pl.when(plain)
            def _():
                big[pl.ds(base, TILE), :] = flat[pl.ds(base, TILE), :].astype(LOW)

            @pl.when(jnp.logical_not(narrow | plain))
            def _():
                for j, part in enumerate(wide_tile(base)):
                    big[pl.ds(base + 16 * j, 16), :] = part

        big[STRIDE * TILE : BIG_ROWS, :] = flat[STRIDE * TILE : BIG_ROWS, :].astype(LOW)

    @pl.when(jnp.logical_not(even))
    def _():
        @pl.loop(0, WINDOW)
        def _(r):
            tile = STRIDE * block + r
            base = pl.multiple_of(TILE * r, TILE)

            @pl.when(tile == VEC_TILE[1])
            def _():
                small[tile] = flat[pl.ds(base, TILE), :].astype(LOW)

            @pl.when(tile < VEC_TILE[1])
            def _():
                for j, part in enumerate(wide_tile(base)):
                    small[tile, 16 * j : 16 * j + 16, :] = part


def prepare(owners, params):
    return pl.pallas_call(
        prepare_kernel,
        name="prepare",
        out_shape=(
            jax.ShapeDtypeStruct((BIG_ROWS, 128), LOW),
            jax.ShapeDtypeStruct((USED_TILES[1], TILE, 128), LOW),
            jax.ShapeDtypeStruct((8, 128), jnp.int32),
        ),
        in_specs=[smem_spec(), any_spec()],
        out_specs=(vmem_spec(),) * 3,
        scratch_shapes=[pltpu.VMEM((WINDOW * TILE, 128), FULL), pltpu.SemaphoreType.DMA],
        compiler_params=pltpu.CompilerParams(vmem_limit_bytes=60 << 20),
    )(owners, params.reshape(-1, 1, 128))


class Place:
    def __init__(self):
        self.dp = lax.axis_index("dp")
        self.pipe = lax.axis_index("pipe")
        self.x, self.core = self.pipe // 2, self.pipe % 2
        self.z, self.y = self.dp // 2, self.dp % 2

    def device(self, x=None, core=None, z=None, y=None):
        x = self.x if x is None else x
        core = self.core if core is None else core
        z = self.z if z is None else z
        y = self.y if y is None else y
        return {"dp": 2 * z + y, "pipe": 2 * x + core}

    def enter(self):
        barrier = pltpu.get_barrier_semaphore()
        for step in range(1, 8):
            other = lax.rem(self.dp + step, 8)
            pl.semaphore_signal(
                barrier, inc=1, device_id={"dp": other, "pipe": self.pipe}, device_id_type=MESH
            )
        for step in range(1, 4):
            other = lax.rem(self.pipe + step, 4)
            pl.semaphore_signal(
                barrier, inc=1, device_id={"dp": self.dp, "pipe": other}, device_id_type=MESH
            )
        pl.semaphore_wait(barrier, 10)


def remote(src, dst, send, recv, target):
    return pltpu.make_async_remote_copy(
        src_ref=src, dst_ref=dst, send_sem=send, recv_sem=recv, device_id=target, device_id_type=MESH
    )


BIG_HALF = BIG_ROWS // 2
SMALL_HALF = SMALL_ROWS // 2
PARTS = 2
PART_ROWS = BIG_HALF // PARTS
BULK_CUT = 480
LIGHT_CUT = 256
BACK_CUT = 720
GATHER_ORDER = (
    "X1", "Z2", "EY", "EC0", "Z3", "Y0", "X2", "EC1", "X3", "Y1", "Y2", "R0", "EC2", "R1", "EC3",
    "Y3", "Z4", "L0", "X4", "Z5", "L1", "S0", "X5", "Y4", "R2", "S1", "L2", "S2", "Y5", "Z6", "R3",
    "Y6", "X6", "S3", "Z7", "Y7", "M1", "S4", "S5", "D0", "D1", "X7", "R4", "S6", "M2", "D2", "S7",
    "D3", "R5", "R6", "R7", "M3", "D4", "D5", "D6", "D7",
)
REDUCE_ORDER = (
    "A0", "A1", "A2", "A3", "A4", "A5", "L0", "A6", "C0", "B0", "C1", "B1", "C2", "L1", "B2", "B3",
    "L2", "L3", "A7", "C3", "O0", "LS", "B4", "C4", "O1", "E0", "C5", "O2", "E1", "B5", "LE", "I0",
    "I1", "B6", "T1", "I2", "C6", "C7", "B7", "E2", "G", "O3", "O4", "I3", "I4", "O5", "T2", "I5",
    "E3", "E4", "E5", "T3", "O6", "O7",
)


def gather_kernel(big, small, ids, all_big, all_small, table, held_big, held_small, k_sem, big_sem, early, chunk, rising, falling,
                  early_send, early_recv, eu_send, eu_recv, ed_send, ed_recv,
                  z_send, z_recv, x_send, x_recv, y_send, y_recv, dx_send, dx_recv, dy_send, dy_recv,
                  s_send, s_recv, first_send, first_recv, own_sem, id_send, id_recv, lz_send, lz_recv):
    me = Place()
    me.enter()
    x, y, z, core = me.x, me.y, me.z, me.core
    up, down = me.device(z=z + 1), me.device(z=z - 1)
    x_side, y_side, sibling = me.device(x=1 - x), me.device(y=1 - y), me.device(core=1 - core)

    class Stream:
        def __init__(self, n, held, out, start, rows, cut):
            self.n, self.held, self.out, self.start, self.rows, self.cut = n, held, out, start, rows, cut

        def block(self, xo, origin, yo):
            return self.held.at[xo, 2 * origin + yo, pl.ds(self.start, self.rows)]

        def move_x(self, origin):
            block = self.block(x, origin, y)
            return remote(block, block, x_send.at[self.n, origin], x_recv.at[self.n, origin], x_side)

        def move_y(self, origin):
            block = self.block(x, origin, y)
            return remote(block, block, y_send.at[self.n, origin], y_recv.at[self.n, origin], y_side)

        def copies(self, xo, origin, yo):
            block, at = self.block(xo, origin, yo), 8 * xo + 2 * origin + yo
            result = self.out.at[xo, 2 * origin + yo, core, pl.ds(self.start, self.rows)]
            return (
                remote(block, result, s_send.at[self.n, at], s_recv.at[self.n, at], sibling),
                pltpu.make_async_copy(block, result, k_sem.at[self.n, at]),
            )

        def share(self, xo, origin, yo):
            for copy in self.copies(xo, origin, yo):
                copy.start()

        def move_z(self, origin, target, way):
            block = self.block(x, origin, y)
            return remote(block, block, z_send.at[self.n, way, origin], z_recv.at[self.n, origin], target)

        def half_x(self, origin, xo, yo):
            part = self.held.at[xo, 2 * origin + yo, pl.ds(self.start + self.cut, self.rows - self.cut)]
            return remote(part, part, dx_send.at[self.n, origin], dx_recv.at[self.n, origin], x_side)

        def half_y(self, origin, xo, yo):
            part = self.held.at[xo, 2 * origin + yo, pl.ds(self.start, self.cut)]
            return remote(part, part, dy_send.at[self.n, origin], dy_recv.at[self.n, origin], y_side)

        def to_x(self, origin):
            self.move_x(origin).start()

        def to_y(self, origin):
            self.move_y(origin).start()

        def from_x(self, origin):
            self.move_x(origin).wait_recv()
            self.half_y(origin, 1 - x, y).start()
            self.share(1 - x, origin, y)

        def from_y(self, origin):
            self.move_y(origin).wait_recv()
            self.half_x(origin, x, 1 - y).start()
            self.share(x, origin, 1 - y)

        def from_diagonal(self, origin):
            self.half_x(origin, 1 - x, 1 - y).wait_recv()
            self.half_y(origin, 1 - x, 1 - y).wait_recv()
            self.share(1 - x, origin, 1 - y)

        def each(self, step, action):
            if step == 0:
                action(z)
            else:
                pl.when(z >= step)(lambda: action(z - step))
                pl.when(z + step <= 3)(lambda: action(z + step))

        def begin(self):
            pl.when(z < 3)(lambda: self.move_z(z, up, 0).start())
            pl.when(z > 0)(lambda: self.move_z(z, down, 1).start())
            self.share(x, z, y)

        def from_z(self, k):
            @pl.when(z >= k)
            def _():
                self.move_z(z - k, up, 0).wait_recv()
                pl.when(z < 3)(lambda: self.move_z(z - k, up, 0).start())
                self.share(x, z - k, y)

            @pl.when(z + k <= 3)
            def _():
                self.move_z(z + k, down, 1).wait_recv()
                pl.when(z > 0)(lambda: self.move_z(z + k, down, 1).start())
                self.share(x, z + k, y)

        def close(self):
            for origin in range(4):
                self.move_x(origin).wait_send()
                self.move_y(origin).wait_send()
                self.half_x(origin, x, 1 - y).wait_send()
                self.half_y(origin, 1 - x, y).wait_send()
                pl.when((z < 3) & (origin <= z))(lambda: self.move_z(origin, up, 0).wait_send())
                pl.when((z > 0) & (origin >= z))(lambda: self.move_z(origin, down, 1).wait_send())
            self.close_shares()

        def close_shares(self):
            for origin in range(4):
                for xo in range(2):
                    for yo in range(2):
                        away, home = self.copies(xo, origin, yo)
                        away.wait_send()
                        home.wait()
                        theirs = self.out.at[xo, 2 * origin + yo, 1 - core, pl.ds(self.start, self.rows)]
                        at = 8 * xo + 2 * origin + yo
                        remote(theirs, theirs, s_send.at[self.n, at], s_recv.at[self.n, at], sibling).wait_recv()

    class Late(Stream):
        def column_z(self, xo, origin, yo, target, way):
            block = self.block(xo, origin, yo)
            at = 2 * xo + yo
            return remote(
                block, block, lz_send.at[way, at, origin], lz_recv.at[at, origin], target
            )

        def leave(self, xo, yo):
            pl.when(z < 3)(lambda: self.column_z(xo, z, yo, up, 0).start())
            pl.when(z > 0)(lambda: self.column_z(xo, z, yo, down, 1).start())
            self.share(xo, z, yo)

        def step(self, k):
            if k == 0:
                self.move_x(z).start()
                self.move_y(z).start()
                self.leave(x, y)
            elif k == 1:
                self.move_x(z).wait_recv()
                self.half_y(z, 1 - x, y).start()
                self.leave(1 - x, y)
                self.move_y(z).wait_recv()
                self.half_x(z, x, 1 - y).start()
                self.leave(x, 1 - y)
            elif k == 2:
                self.half_x(z, 1 - x, 1 - y).wait_recv()
                self.half_y(z, 1 - x, 1 - y).wait_recv()
                self.leave(1 - x, 1 - y)
            else:
                gap = k - 2

                @pl.when(z >= gap)
                def _():
                    for xo, yo in columns:
                        self.column_z(xo, z - gap, yo, up, 0).wait_recv()
                        pl.when(z < 3)(lambda: self.column_z(xo, z - gap, yo, up, 0).start())
                        self.share(xo, z - gap, yo)

                @pl.when(z + gap <= 3)
                def _():
                    for xo, yo in columns:
                        self.column_z(xo, z + gap, yo, down, 1).wait_recv()
                        pl.when(z > 0)(lambda: self.column_z(xo, z + gap, yo, down, 1).start())
                        self.share(xo, z + gap, yo)

        def close(self):
            self.move_x(z).wait_send()
            self.move_y(z).wait_send()
            self.half_x(z, x, 1 - y).wait_send()
            self.half_y(z, 1 - x, y).wait_send()
            for origin in range(4):
                for xo, yo in columns:
                    pl.when((z < 3) & (origin <= z))(
                        lambda: self.column_z(xo, origin, yo, up, 0).wait_send())
                    pl.when((z > 0) & (origin >= z))(
                        lambda: self.column_z(xo, origin, yo, down, 1).wait_send())
            self.close_shares()

    columns = ((x, y), (1 - x, y), (x, 1 - y), (1 - x, 1 - y))
    bulks = [
        Stream(n, held_big, all_big, PART_ROWS * n, PART_ROWS, BULK_CUT) for n in range(PARTS)
    ]
    light = Late(PARTS, held_small, all_small, 0, SMALL_HALF, LIGHT_CUT)

    order = [
        jnp.where(z < 2, 3, 0),
        jnp.where(z == 0, 2, jnp.where(z == 1, 0, jnp.where(z == 2, 3, 1))),
        jnp.where(z == 0, 1, jnp.where(z == 1, 2, jnp.where(z == 2, 1, 2))),
        z,
    ]

    def cross(k):
        return remote(small.at[2 * order[k] + (1 - y)], early.at[k], early_send.at[k], early_recv.at[k], y_side)

    def own_early(k):
        return pltpu.make_async_copy(small.at[2 * order[k] + y], chunk.at[k], own_sem.at[3 + k])

    def rise(k):
        slot = order[k] - 1
        return remote(chunk.at[k], rising.at[slot], eu_send.at[slot], eu_recv.at[slot], up)

    def fall(k):
        slot = order[k]
        return remote(chunk.at[k], falling.at[slot], ed_send.at[slot], ed_recv.at[slot], down)

    def merge(k, ref, slot):
        @pl.loop(0, 3)
        def _(i):
            part = pl.ds(pl.multiple_of(352 * i, 16), 352)
            chunk[k, part, :] = (chunk[k, part, :].astype(FULL) + ref[slot, part, :].astype(FULL)).astype(LOW)

    def big_part(n):
        return held_big.at[x, me.dp, pl.ds(PART_ROWS * n, PART_ROWS)]

    def big_first(n):
        source = big.at[pl.ds(BIG_HALF + PART_ROWS * n, PART_ROWS)]
        return remote(source, big_part(n), first_send.at[n], first_recv.at[n], sibling)

    def big_own(n):
        return pltpu.make_async_copy(big.at[pl.ds(PART_ROWS * n, PART_ROWS)], big_part(n), big_sem.at[n])

    small_half = held_small.at[x, me.dp]
    small_first = remote(
        chunk.at[3, pl.ds(0, SMALL_HALF)], small_half, first_send.at[PARTS], first_recv.at[PARTS], sibling)

    def early_cross():
        @pl.when(core == 1)
        def _():
            for k in range(4):
                own_early(k).wait()
                cross(k).wait_recv()
                merge(k, early, k)

    def early_chain(k):
        @pl.when(core == 1)
        def _():
            if k < 3:

                @pl.when(order[k] > z)
                def _():
                    @pl.when(z > 0)
                    def _():
                        rise(k).wait_recv()
                        merge(k, rising, order[k] - 1)

                    rise(k).start()

                @pl.when(order[k] < z)
                def _():
                    @pl.when(z < 3)
                    def _():
                        fall(k).wait_recv()
                        merge(k, falling, order[k])

                    fall(k).start()

            else:

                @pl.when(z > 0)
                def _():
                    rise(k).wait_recv()
                    merge(k, rising, z - 1)

                @pl.when(z < 3)
                def _():
                    fall(k).wait_recv()
                    merge(k, falling, z)

                small_first.start()
                copy = pltpu.make_async_copy(
                    chunk.at[3, pl.ds(SMALL_HALF, SMALL_HALF)], small_half, own_sem.at[0])
                copy.start()
                copy.wait()

    def light_begin():
        @pl.when(core == 0)
        def _():
            small_first.wait_recv()

        light.step(0)

    @pl.when(core == 0)
    def _():
        for n in range(PARTS):
            big_first(n).start()
            big_own(n).start()

    @pl.when(core == 1)
    def _():
        for k in range(4):
            cross(k).start()
            own_early(k).start()

    for n in range(PARTS):
        pl.when(core == 0)(lambda: big_own(n).wait())
        pl.when(core == 1)(lambda: big_first(n).wait_recv())
        bulks[n].begin()
        if n == 0:
            bulks[n].to_x(z)
    row = pltpu.make_async_copy(ids, table.at[me.pipe], own_sem.at[2])
    row.start()
    for step in range(1, 4):
        remote(
            ids, table.at[me.pipe], id_send.at[step], id_recv.at[step],
            {"dp": me.dp, "pipe": lax.rem(me.pipe + step, 4)},
        ).start()

    actions = {"EY": early_cross, "L0": light_begin}
    for k in range(4):
        actions["EC%d" % k] = functools.partial(early_chain, k)
        if k:
            actions["M%d" % k] = functools.partial(light.step, k + 2)
            if k < 3:
                actions["L%d" % k] = functools.partial(light.step, k)
        for n, bulk in enumerate(bulks):
            name = str(PARTS * k + n)
            for letter, action in zip("XYSRD", (bulk.to_x, bulk.to_y, bulk.from_x, bulk.from_y, bulk.from_diagonal)):
                actions[letter + name] = functools.partial(bulk.each, k, action)
            if k:
                actions["Z" + name] = functools.partial(bulk.from_z, k)
    for event in GATHER_ORDER:
        actions[event]()
    for bulk in bulks:
        bulk.close()
    light.close()
    row.wait()
    for step in range(1, 4):
        here = lax.rem(me.pipe + 4 - step, 4)
        move = remote(
            ids, table.at[here], id_send.at[step], id_recv.at[step],
            {"dp": me.dp, "pipe": lax.rem(me.pipe + step, 4)},
        )
        move.wait_recv()
        move.wait_send()

    @pl.when(core == 0)
    def _():
        for n in range(PARTS):
            big_first(n).wait_send()

    @pl.when(core == 1)
    def _():
        small_first.wait_send()
        for k in range(4):
            cross(k).wait_send()
        for k in range(3):
            pl.when(order[k] > z)(lambda: rise(k).wait_send())
            pl.when(order[k] < z)(lambda: fall(k).wait_send())


def gather_all(big, small, ids):
    sem = pltpu.SemaphoreType.DMA
    return pl.pallas_call(
        gather_kernel,
        name="gather_all",
        out_shape=(
            jax.ShapeDtypeStruct((2, 8, 2, BIG_HALF, 128), LOW),
            jax.ShapeDtypeStruct((2, 8, 2, SMALL_HALF, 128), LOW),
            jax.ShapeDtypeStruct((4, 8, 128), jnp.int32),
        ),
        in_specs=[any_spec()] * 3,
        out_specs=(any_spec(),) * 3,
        scratch_shapes=[
            pltpu.VMEM((2, 8, BIG_HALF, 128), LOW), pltpu.VMEM((2, 8, SMALL_HALF, 128), LOW),
            sem((PARTS + 1, 16)), sem((PARTS,)),
            pltpu.VMEM((4, SMALL_ROWS, 128), LOW), pltpu.VMEM((4, SMALL_ROWS, 128), LOW),
            pltpu.VMEM((3, SMALL_ROWS, 128), LOW), pltpu.VMEM((3, SMALL_ROWS, 128), LOW),
            sem((4,)), sem((4,)), sem((3,)), sem((3,)), sem((3,)), sem((3,)),
            sem((PARTS + 1, 2, 4)), sem((PARTS + 1, 4)),
            sem((PARTS + 1, 4)), sem((PARTS + 1, 4)), sem((PARTS + 1, 4)), sem((PARTS + 1, 4)),
            sem((PARTS + 1, 4)), sem((PARTS + 1, 4)), sem((PARTS + 1, 4)), sem((PARTS + 1, 4)),
            sem((PARTS + 1, 16)), sem((PARTS + 1, 16)),
            sem((PARTS + 1,)), sem((PARTS + 1,)), sem((7,)), sem((4,)), sem((4,)),
            sem((2, 4, 4)), sem((4, 4)),
        ],
        compiler_params=pltpu.CompilerParams(
            collective_id=0, has_side_effects=True, vmem_limit_bytes=60 << 20
        ),
    )(big, small.reshape(8, SMALL_ROWS, 128), ids)


def soft(value):
    return jnp.maximum(value, 0.0) + jnp.log1p(jnp.exp(-jnp.abs(value)))


def gate_of(value):
    small = jnp.exp(-jnp.abs(value))
    share = 1.0 / (1.0 + small)
    return jnp.where(value >= 0, share, small * share)


def standardize(z):
    count = z.shape[0]
    centre = jnp.sum(z, axis=0, keepdims=True) / count
    away = z - centre
    spread = jnp.sum(away * away, axis=0, keepdims=True) / count
    inverse = lax.rsqrt(spread + NORM_EPS)
    return away * inverse, centre, spread, inverse


def unstandardize(grad, standard, gain, inverse):
    count = grad.shape[0]
    grad_sum = jnp.sum(grad, axis=0, keepdims=True)
    grad_dot = jnp.sum(grad * standard, axis=0, keepdims=True)
    result = gain * inverse * (grad - grad_sum / count - standard * (grad_dot / count))
    return result, grad_dot, grad_sum


def pad_low(value):
    zeros = jnp.zeros((PADDED - ROWS, value.shape[1]), FULL)
    return jnp.concatenate([value, zeros], axis=0).astype(LOW)


def mul(a, b):
    return jnp.dot(a, b, preferred_element_type=FULL)


def mul_t(a, b):
    return lax.dot_general(a, b, (((1,), (1,)), ((), ())), preferred_element_type=FULL)


def narrow_part(ref, start, count, blocks=range(4)):
    return jnp.concatenate(
        [ref[pl.ds(start, count), 64 * j : 64 * j + 64, :].reshape(64 * count, 128) for j in blocks],
        axis=1,
    )


def put_narrow(ref, start, count, value):
    for j in range(4):
        ref[pl.ds(start, count), 64 * j : 64 * j + 64, :] = (
            value[:, 128 * j : 128 * j + 128].astype(LOW).reshape(count, 64, 128)
        )


def wide_part(ref, start, count, c):
    return jnp.concatenate(
        [
            ref[start : start + count, 32 * c + 16 * h : 32 * c + 16 * h + 16, :].reshape(
                16 * count, 128
            )
            for h in range(2)
        ],
        axis=1,
    )


def put_wide(ref, start, count, c, value):
    for h in range(2):
        ref[start : start + count, 32 * c + 16 * h : 32 * c + 16 * h + 16, :] = (
            value[:, 128 * h : 128 * h + 128].astype(LOW).reshape(count, 16, 128)
        )


def chunks(count):
    def run(body):
        for c in range(count):
            body(c)

    return run


def step_kernel(table, gates, teach_ids, stud_ids, all_big, all_small, x, targets, grid,
                wide0, wide1, final, stats, grad_x, out_big, out_small,
                w0, w1, w2, w3, edges, loose, vec, grad_vec, raw,
                std_a, std_b, std_p, std_1, std_c, std_d, hidden, cols0, cols2,
                nar0, nar2, turned, turned_x, relay, dz_a, dz_n, acc, acc_x, grad_h,
                wanted, inv, in_sem, edge_sem, out_sem):
    rank = lax.axis_index("pipe")
    gate = gates[rank].astype(FULL)
    for group in range(2):
        for j in range(8):
            inv[8 * group + table[2 * group, 0, j]] = j
    picks = [teach_ids[k, rank] for k in range(2)] + [stud_ids[rank, k] for k in range(3)]
    rows = [
        pltpu.make_async_copy(targets.at[pl.ds(pick, 1)], wanted.at[pl.ds(k, 1)], edge_sem.at[12 + k])
        for k, pick in enumerate(picks)
    ]
    for fetched in rows:
        fetched.start()
    weights = (w0, w1, w2, w3)
    loads = {0: [], 1: [], 2: [], 3: []}
    front, split = w0.reshape(USED_TILES[0] * TILE, 128), w2.reshape(115 * TILE, 128)
    for group, weight, blocks in ((0, front, 8), (1, split, 6)):
        for b in range(blocks):
            at, here = 8 * group + b, inv[8 * group + b]
            count = min(STRIDE, VEC_TILE[2 * group] + 1 - STRIDE * b) * TILE
            loads[2 * group].append(pltpu.make_async_copy(
                all_big.at[group, here, pl.ds(0, count)], weight.at[pl.ds(STRIDE * TILE * b, count)],
                in_sem.at[0, at]))
            if b < blocks - 1:
                loads[2 * group].append(pltpu.make_async_copy(
                    all_big.at[group, here, pl.ds(STRIDE * TILE, EDGE)], edges.at[7 * group + b],
                    edge_sem.at[7 * group + b]))
            elif group == 0:
                loads[0].append(pltpu.make_async_copy(
                    all_big.at[0, here, pl.ds(STRIDE * TILE, EDGE)],
                    front.at[pl.ds(VEC_TILE[0] * TILE, EDGE)], edge_sem.at[17]))
    loads[1].append(pltpu.make_async_copy(all_small.at[0], w1, in_sem.at[0, 14]))
    loads[3].append(pltpu.make_async_copy(all_small.at[1], w3, in_sem.at[0, 15]))
    for section in range(4):
        for load in loads[section]:
            load.start()

    raw[...] = jnp.zeros_like(raw)
    loose[...] = jnp.zeros_like(loose)
    grad_vec[...] = jnp.zeros_like(grad_vec)

    def edge_parts(tile, is_narrow):
        count, size = (4, 64) if is_narrow else (16, 16)
        for j in range(count):
            yield pl.ds(j, 16, count), slice(size * j, size * j + 16)

    def is_narrow(section, tile):
        return section == 2 or tile < FRONT_WIDE

    def merge_edge(section, tile, at):
        ref = weights[section]
        loose[0:EDGE, :] = edges[at].astype(FULL)
        for lying, here in edge_parts(tile, is_narrow(section, tile)):
            ref[tile, here, :] = (ref[tile, here, :].astype(FULL) + loose[lying, :]).astype(LOW)

    def take_edge(section, tile, at):
        ref = weights[section]
        for lying, here in edge_parts(tile, is_narrow(section, tile)):
            loose[lying, :] = ref[tile, here, :].astype(FULL)
        edges[at] = loose[0:EDGE, :].astype(LOW)

    def settle(section, blocks=None):
        if section == 0:
            for b in blocks:
                for load in loads[0][2 * b : 2 * b + 2]:
                    load.wait()
            if 7 in blocks:
                vec[0] = w0[VEC_TILE[0], 0:48, :].astype(FULL)
            else:
                for b in range(7):
                    merge_edge(0, 19 * b + 19, b)
            return
        for load in loads[section]:
            load.wait()
        if section == 2:
            for b in range(5):
                merge_edge(2, 19 * b + 19, 7 + b)
        vec[section] = weights[section][VEC_TILE[section], 0:48, :].astype(FULL)

    def row(section, start):
        return jnp.concatenate(
            [vec[section, pl.ds(start + h, 1), :] for h in range(2)], axis=1
        )

    def put_row(section, start, value):
        for h in range(2):
            grad_vec[section, pl.ds(start + h, 1), :] = value[:, 128 * h : 128 * h + 128]

    def put_stats(section, column, centre, spread):
        raw[2 * section : 2 * section + 1, pl.ds(column, 256)] = centre
        raw[2 * section + 1 : 2 * section + 2, pl.ds(column, 256)] = spread

    def inverse_of(section, column):
        return lax.rsqrt(raw[2 * section + 1 : 2 * section + 2, pl.ds(column, 256)] + NORM_EPS)

    def lanes(c):
        return slice(256 * c, 256 * c + 256)

    at_row, at_col, side = grid[0], grid[1], grid[2]

    def masked(value, dr, dc):
        ok = (at_row + dr >= 0) & (at_row + dr < side) & (at_col + dc >= 0) & (at_col + dc < side)
        return jnp.concatenate(
            [jnp.where(ok, value[:, 128 * j : 128 * j + 128], 0.0) for j in range(4)], axis=1
        )

    def rolled(value, sign, dr, dc):
        parts = []
        for start, end, across, down in ((0, STUD_ROWS, 1, 4), (STUD_ROWS, ROWS, 2, 12)):
            by = (sign * (dr * down + dc * across)) % (end - start)
            part = value[start:end]
            parts.append(part if by == 0 else pltpu.roll(part, by, 0))
        return jnp.concatenate(parts, axis=0)

    def taps(stride):
        for t in range(9):
            r, q = t // 3, t % 3
            if stride == 1:
                yield t, 0, r - 1, q - 1
            else:
                phase = 2 * (1 if r != 1 else 0) + (1 if q != 1 else 0)
                yield t, phase, -1 if r == 0 else 0, -1 if q == 0 else 0

    settle(0, (0, 7))
    whole_x = x[...].reshape(4 * PADDED, C_IN)
    for c in range(2):
        z = mul(whole_x, narrow_part(w0, 0, 16, (2 * c, 2 * c + 1)))
        z = jnp.concatenate([z[PADDED * p : PADDED * p + ROWS] for p in range(4)], axis=0)
        standard, centre, spread, _ = standardize(z)
        put_stats(0, 256 * c, centre, spread)
        std_a[:, 256 * c : 256 * c + 256] = standard
        hidden[:, 256 * c : 256 * c + 256] = (
            soft(row(0, 2 * c) * standard + row(0, 4 + 2 * c)).astype(LOW).astype(FULL)
        )

    for t, phase, dr, dc in taps(2):
        cols0[t] = pad_low(masked(rolled(hidden[ROWS * phase : ROWS * phase + ROWS, :], -1, dr, dc), dr, dc))
    acc[...] = jnp.zeros_like(acc)
    settle(0, (1, 2, 3, 4, 5, 6))

    @chunks(9)
    def _(t):
        acc[...] += mul(cols0[t], narrow_part(w0, 16 + 8 * t, 8))

    def middle(section, std, nar):
        for c in range(2):
            at = slice(256 * c, 256 * c + 256)
            standard, centre, spread, _ = standardize(acc[0:ROWS, at])
            put_stats(section, MID + 256 * c, centre, spread)
            std[:, at] = standard
            nar[:, at] = pad_low(soft(row(section, 8 + 2 * c) * standard + row(section, 12 + 2 * c)))

    middle(0, std_b, nar0)
    acc[...] = jnp.zeros_like(acc)
    settle(1)
    settle(2)

    @chunks(8)
    def _(c):
        at = lanes(c)
        standard, centre, spread, _ = standardize(mul(x[0], wide_part(w0, FRONT_WIDE, 64, c))[0:ROWS])
        put_stats(0, 2 * MID + 256 * c, centre, spread)
        std_p[:, at] = standard
        low = pad_low(row(0, 16 + 2 * c) * standard + row(0, 32 + 2 * c))
        wide0[:, at] = low
        standard, centre, spread, _ = standardize(mul(nar0[...], wide_part(w1, 0, 32, c))[0:ROWS])
        put_stats(1, 256 * c, centre, spread)
        std_1[:, at] = standard
        pre = low.astype(FULL)[0:ROWS] + row(1, 2 * c) * standard + row(1, 16 + 2 * c)
        low = pad_low(soft(pre))
        wide1[:, at] = low
        acc[...] += mul(low, narrow_part(w2, 4 * c, 4))

    for c in range(2):
        at = slice(256 * c, 256 * c + 256)
        standard, centre, spread, _ = standardize(acc[0:ROWS, at])
        put_stats(2, 256 * c, centre, spread)
        std_c[:, at] = standard
        hidden[0:ROWS, at] = soft(row(2, 2 * c) * standard + row(2, 4 + 2 * c)).astype(LOW).astype(FULL)
    for t, phase, dr, dc in taps(1):
        cols2[t] = pad_low(masked(rolled(hidden[0:ROWS, :], -1, dr, dc), dr, dc))
    acc[...] = jnp.zeros_like(acc)

    @chunks(9)
    def _(t):
        acc[...] += mul(cols2[t], narrow_part(w2, 32 + 8 * t, 8))

    middle(2, std_d, nar2)

    turned[...] = nar2[...].T
    acc[...] = jnp.zeros_like(acc)
    settle(3)
    for fetched in rows:
        fetched.wait()

    teach_rows = ROWS - STUD_ROWS
    first_crop = lax.rem(lax.broadcasted_iota(jnp.int32, (teach_rows, 256), 0), 2) == 0

    def spread_rows(values):
        first, second = (jnp.broadcast_to(value, (teach_rows, 256)) for value in values[0:2])
        parts = [jnp.broadcast_to(value, (16, 256)) for value in values[2:5]]
        parts.append(jnp.where(first_crop, first, second))
        return jnp.concatenate(parts, axis=0)

    def crop_sums(value):
        def total(part):
            return jnp.sum(part, axis=0, keepdims=True)

        teach = value[STUD_ROWS:ROWS]
        return [
            total(jnp.where(first_crop, teach, 0.0)),
            total(jnp.where(first_crop, 0.0, teach)),
            total(value[0:16]),
            total(value[16:32]),
            total(value[32:48]),
        ]

    @chunks(8)
    def _(c):
        at = lanes(c)
        weight = wide_part(w3, 0, 32, c)
        standard, centre, spread, inverse = standardize(mul(nar2[...], weight)[0:ROWS])
        put_stats(3, 256 * c, centre, spread)
        gain = row(3, 2 * c)
        before = wide1[:, at].astype(FULL)[0:ROWS]
        pre = before + gain * standard + row(3, 16 + 2 * c)
        ending = jnp.where(gate > 0, soft(pre), before)
        final[:, at] = pad_low(ending)
        square = ending * ending
        factors = []
        for crop, total in enumerate(crop_sums(square * ending)):
            mean = total / (36.0 if crop < 2 else 16.0) + POOL_EPS
            factors.append(jnp.exp(jnp.log(mean) * (-2.0 / 3.0)) * wanted[crop : crop + 1, at])
        cotangent = spread_rows(factors) * square
        grad_pre = cotangent * gate_of(pre) * gate
        relay[:, at] = pad_low(grad_pre + cotangent * (1.0 - gate))
        result, grad_gain, grad_bias = unstandardize(grad_pre, standard, gain, inverse)
        put_row(3, 2 * c, grad_gain)
        put_row(3, 16 + 2 * c, grad_bias)
        low = pad_low(result)
        acc[...] += mul_t(low, weight)
        put_wide(w3, 0, 32, c, mul(turned[...], low))

    def flush(section):
        weights[section][VEC_TILE[section]] = grad_vec[section].astype(LOW)

    flush(3)
    stores = [pltpu.make_async_copy(w3, out_small.at[1], out_sem.at[16])]
    stores[-1].start()

    def middle_back(section, std):
        for c in range(2):
            at = slice(256 * c, 256 * c + 256)
            gain, bias = row(section, 8 + 2 * c), row(section, 12 + 2 * c)
            grad = acc[0:ROWS, at].astype(LOW).astype(FULL) * gate_of(gain * std[:, at] + bias)
            result, grad_gain, grad_bias = unstandardize(
                grad, std[:, at], gain, inverse_of(section, MID + 256 * c)
            )
            put_row(section, 8 + 2 * c, grad_gain)
            put_row(section, 12 + 2 * c, grad_bias)
            dz_n[:, at] = pad_low(result)

    def taps_back(weight, start, cols, stride, phases):
        grad_h[0 : ROWS * phases, :] = jnp.zeros((ROWS * phases, MID), FULL)
        for t, phase, dr, dc in taps(stride):
            part = mul_t(dz_n[...], narrow_part(weight, start + 8 * t, 8))[0:ROWS]
            at = slice(ROWS * phase, ROWS * phase + ROWS)
            grad_h[at, :] += rolled(masked(part, dr, dc), 1, dr, dc)
            put_narrow(weight, start + 8 * t, 8, mul(cols[t].T, dz_n[...]))

    middle_back(2, std_d)
    taps_back(w2, 32, cols2, 1, 1)
    for c in range(2):
        at = slice(256 * c, 256 * c + 256)
        gain, bias = row(2, 2 * c), row(2, 4 + 2 * c)
        grad = grad_h[0:ROWS, at] * gate_of(gain * std_c[:, at] + bias)
        result, grad_gain, grad_bias = unstandardize(grad, std_c[:, at], gain, inverse_of(2, 256 * c))
        put_row(2, 2 * c, grad_gain)
        put_row(2, 4 + 2 * c, grad_bias)
        dz_n[:, at] = pad_low(result)
    turned[...] = nar0[...].T
    turned_x[...] = x[0].T
    acc[...] = jnp.zeros_like(acc)
    acc_x[...] = jnp.zeros_like(acc_x)

    @chunks(8)
    def _(c):
        at = lanes(c)
        low = dz_n[...]
        grad = relay[:, at].astype(FULL) + mul_t(low, narrow_part(w2, 4 * c, 4))
        put_narrow(w2, 4 * c, 4, mul(wide1[:, at].T, low))
        grad = grad.astype(LOW).astype(FULL)[0:ROWS]
        gain = row(1, 2 * c)
        pre = wide0[:, at].astype(FULL)[0:ROWS] + gain * std_1[:, at] + row(1, 16 + 2 * c)
        grad = grad * gate_of(pre)
        result, grad_gain, grad_bias = unstandardize(
            grad, std_1[:, at], gain, inverse_of(1, 256 * c)
        )
        put_row(1, 2 * c, grad_gain)
        put_row(1, 16 + 2 * c, grad_bias)
        low = pad_low(result)
        acc[...] += mul_t(low, wide_part(w1, 0, 32, c))
        put_wide(w1, 0, 32, c, mul(turned[...], low))
        grad = grad.astype(LOW).astype(FULL)
        result, grad_gain, grad_bias = unstandardize(
            grad, std_p[:, at], row(0, 16 + 2 * c), inverse_of(0, 2 * MID + 256 * c)
        )
        put_row(0, 16 + 2 * c, grad_gain)
        put_row(0, 32 + 2 * c, grad_bias)
        low = pad_low(result)
        acc_x[...] += mul_t(low, wide_part(w0, FRONT_WIDE, 64, c))
        put_wide(w0, FRONT_WIDE, 64, c, mul(turned_x[...], low))

    flush(1)
    flush(2)
    w2[105:115] = jnp.zeros((10, TILE, 128), LOW)
    stores.append(pltpu.make_async_copy(w1, out_small.at[0], out_sem.at[17]))
    stores[-1].start()
    def store(source, group, b, start, semaphore):
        count = source.shape[0]
        stores.append(pltpu.make_async_copy(
            source, out_big.at[group, inv[8 * group + b], pl.ds(start, count)], out_sem.at[semaphore]))
        stores[-1].start()

    for b in range(8):
        if b < 5:
            take_edge(2, 19 * b + 19, 7 + b)
            store(split.at[pl.ds(STRIDE * TILE * b, STRIDE * TILE)], 1, b, 0, 8 + b)
            store(edges.at[7 + b], 1, b, STRIDE * TILE, 20 + b)
        else:
            first = 95 if b == 5 else 105
            store(split.at[pl.ds(TILE * first, 10 * TILE)], 1, b, 0, 8 + b)
            store(split.at[pl.ds(TILE * 105, BIG_ROWS - 10 * TILE)], 1, b, 10 * TILE, 20 + b)

    def store_front(blocks):
        for b in blocks:
            if b == 7:
                edges[12] = w0[VEC_TILE[0], 0:EDGE, :]
            else:
                take_edge(0, 19 * b + 19, b)
            store(front.at[pl.ds(STRIDE * TILE * b, STRIDE * TILE)], 0, b, 0, b)
            store(edges.at[12 if b == 7 else b], 0, b, STRIDE * TILE, 28 + b)

    store_front((5, 6))
    middle_back(0, std_b)
    taps_back(w0, 16, cols0, 2, 4)
    store_front((1, 2, 3, 4))
    for c in range(2):
        at = slice(256 * c, 256 * c + 256)
        gain, bias = row(0, 2 * c), row(0, 4 + 2 * c)
        grad = grad_h[:, at] * gate_of(gain * std_a[:, at] + bias)
        result, grad_gain, grad_bias = unstandardize(grad, std_a[:, at], gain, inverse_of(0, 256 * c))
        put_row(0, 2 * c, grad_gain)
        put_row(0, 4 + 2 * c, grad_bias)
        for p in range(4):
            dz_a[PADDED * p : PADDED * p + PADDED, at] = pad_low(result[ROWS * p : ROWS * p + ROWS])

    @chunks(4)
    def _(c):
        at = lanes(c)
        low = dz_a[...]
        part = mul_t(low, narrow_part(w0, 4 * c, 4))
        grad_x[0, :, at] = (part[0:PADDED] + acc_x[:, at]).astype(LOW)
        for p in range(1, 4):
            grad_x[p, :, at] = part[PADDED * p : PADDED * p + PADDED].astype(LOW)
        put_narrow(w0, 4 * c, 4, mul(x[:, :, at].reshape(4 * PADDED, 256).T, low))

    flush(0)
    store_front((0, 7))
    for section in range(4):
        part = raw[2 * section : 2 * section + 2]
        stats[section, 0:2] = part if section < 2 else part * gate
        stats[section, 2:8] = jnp.zeros((6, 2 * MID + C_OUT), FULL)
    for store in stores:
        store.wait()


def run_step(table, gates, teach_ids, stud_ids, all_big, all_small, phases, targets):
    spots = np.zeros((3, ROWS, 128), np.int32)
    for r in range(ROWS):
        width = 4 if r < STUD_ROWS else 6
        at = r % 16 if r < STUD_ROWS else (r - STUD_ROWS) // 2
        spots[0, r], spots[1, r], spots[2, r] = at // width, at % width, width
    sem = pltpu.SemaphoreType.DMA
    wide = jax.ShapeDtypeStruct((PADDED, C_OUT), LOW)
    vm = pltpu.VMEM
    return pl.pallas_call(
        step_kernel,
        name="step",
        out_shape=(
            wide, wide, wide,
            jax.ShapeDtypeStruct((4, 8, 2 * MID + C_OUT), FULL),
            jax.ShapeDtypeStruct((4, PADDED, C_IN), LOW),
            jax.ShapeDtypeStruct((2, 8, BIG_ROWS, 128), LOW),
            jax.ShapeDtypeStruct((2, USED_TILES[1], TILE, 128), LOW),
        ),
        in_specs=[smem_spec()] * 4 + [any_spec(), any_spec(), vmem_spec(), any_spec(), vmem_spec()],
        out_specs=(vmem_spec(),) * 5 + (any_spec(),) * 2,
        scratch_shapes=[
            vm((153, TILE, 128), LOW), vm((33, TILE, 128), LOW), vm((115, TILE, 128), LOW), vm((33, TILE, 128), LOW),
            vm((13, EDGE, 128), LOW), vm((TILE, 128), FULL), vm((4, 48, 128), FULL), vm((4, TILE, 128), FULL),
            vm((8, 2 * MID + C_OUT), FULL),
            vm((4 * ROWS, MID), FULL), vm((ROWS, MID), FULL), vm((ROWS, C_OUT), FULL), vm((ROWS, C_OUT), FULL),
            vm((ROWS, MID), FULL), vm((ROWS, MID), FULL), vm((4 * ROWS, MID), FULL),
            vm((9, PADDED, MID), LOW), vm((9, PADDED, MID), LOW),
            vm((PADDED, MID), LOW), vm((PADDED, MID), LOW), vm((MID, PADDED), LOW), vm((C_IN, PADDED), LOW),
            vm((PADDED, C_OUT), LOW), vm((4 * PADDED, MID), LOW), vm((PADDED, MID), LOW),
            vm((PADDED, MID), FULL), vm((PADDED, C_IN), FULL), vm((4 * ROWS, MID), FULL),
            vm((8, C_OUT), FULL), pltpu.SMEM((16,), jnp.int32),
            sem((2, 16)), sem((18,)), sem((36,)),
        ],
        compiler_params=pltpu.CompilerParams(vmem_limit_bytes=60 << 20),
    )(table, gates, teach_ids, stud_ids, all_big, all_small, phases, targets, jnp.asarray(spots))


def reduce_kernel(big, small, wide0, wide1, final, stats, table,
                  out_big, out_small, seg_stud, seg_teach, out_stats, norm, factor,
                  got, halves_x, halves_y, from_x, from_y, from_low, from_high, stage, total,
                  l_got, l_stage, l_low, l_high, l_halves_x, l_halves_y, l_from_x, l_from_y, l_total,
                  late, late_half, owner_row, by_pipe, by_dp, mine, part_sum,
                  s_send, s_recv, ls_send, ls_recv, hx_send, hx_recv, hy_send, hy_recv, x_send, x_recv, y_send, y_recv,
                  zu_send, zu_recv, zd_send, zd_recv, lu_send, lu_recv, ld_send, ld_recv,
                  stage_sem, l_stage_sem, out_sem, big_sem, late_send, late_recv, join_send, join_recv,
                  seg_send, seg_recv, stat_send, stat_recv, p_send, p_recv, d_send, d_recv):
    me = Place()
    me.enter()
    x, y, z, core = me.x, me.y, me.z, me.core
    up, down = me.device(z=z + 1), me.device(z=z - 1)
    x_side, y_side, sibling = me.device(x=1 - x), me.device(y=1 - y), me.device(core=1 - core)
    order = [
        jnp.where(z < 2, 3, 0),
        jnp.where(z == 0, 2, jnp.where(z == 1, 0, jnp.where(z == 2, 3, 1))),
        jnp.where(z == 0, 1, jnp.where(z == 1, 2, jnp.where(z == 2, 1, 2))),
        z,
    ]
    columns = ((1 - x, 1 - y), (x, 1 - y), (1 - x, y), (x, y))
    groups = {"A": (0,), "C": (1,), "B": (2,), "O": (3,)}
    sequence = [
        (group, int(event[1])) for event in REDUCE_ORDER for group in groups.get(event[0], ())
    ]
    l_sequence = [(group, k) for k in range(4) for group in range(4)]

    def all_of(copies, act):
        for copy in copies:
            act(copy)

    def over(start, count, piece):
        whole = count // 512
        if whole:

            @pl.loop(0, whole)
            def _(i):
                piece(pl.multiple_of(start + 512 * i, 16), 512)

        if count % 512:
            piece(start + 512 * whole, count % 512)

    items = 4 * PARTS

    def source(group, q, half):
        xo, yo = columns[group]
        part = pl.ds(PART_ROWS * (q % PARTS), PART_ROWS)
        return big.at[xo, 2 * order[q // PARTS] + yo, half, part]

    def l_source(group, k, half):
        xo, yo = columns[group]
        return small.at[xo, 2 * order[k] + yo, half]

    def share(group, q):
        at = items * group + q
        return remote(source(group, q, 1 - core), got.at[at], s_send.at[at], s_recv.at[at], sibling)

    def l_share(group, k):
        at = 4 * group + k
        return remote(l_source(group, k, 1 - core), l_got.at[at], ls_send.at[at], ls_recv.at[at], sibling)

    def fetch(n):
        return pltpu.make_async_copy(source(*sequence[n], core), stage.at[n % 4], stage_sem.at[n % 4])

    def l_fetch(group, k):
        at = 4 * group + k
        return pltpu.make_async_copy(l_source(group, k, core), l_stage.at[at], l_stage_sem.at[at])

    def add(target, at, other, slot, start, count, extras):
        def piece(begin, size):
            part = pl.ds(begin, size)
            sums = target[at, part, :].astype(FULL) + other[slot, part, :].astype(FULL)
            for ref, k in extras:
                sums = sums + ref[k, pl.ds(begin - start, size), :].astype(FULL)
            target[at, part, :] = sums.astype(LOW)

        over(start, count, piece)

    def send_half_x(k):
        return remote(got.at[k, pl.ds(BACK_CUT, PART_ROWS - BACK_CUT)], halves_x.at[k],
                      hx_send.at[k], hx_recv.at[k], x_side)

    def send_half_y(k):
        return remote(got.at[k, pl.ds(0, BACK_CUT)], halves_y.at[k], hy_send.at[k], hy_recv.at[k], y_side)

    def send_y(k):
        return remote(got.at[items + k], from_y.at[k], y_send.at[k], y_recv.at[k], y_side)

    def send_x(k):
        return remote(got.at[2 * items + k], from_x.at[k], x_send.at[k], x_recv.at[k], x_side)

    def low_slot(q):
        return PARTS * (order[q // PARTS] - 1) + q % PARTS

    def high_slot(q):
        return PARTS * order[q // PARTS] + q % PARTS

    def send_up(q):
        slot = low_slot(q)
        return remote(got.at[3 * items + q], from_low.at[slot], zu_send.at[slot], zu_recv.at[slot], up)

    def send_down(q):
        slot = high_slot(q)
        return remote(got.at[3 * items + q], from_high.at[slot], zd_send.at[slot], zd_recv.at[slot], down)

    def l_column(group):
        xo, yo = columns[group]
        return 2 * xo + yo

    def l_up(group, k):
        at, zd = l_column(group), order[k] - 1
        return remote(l_got.at[4 * group + k], l_low.at[at, zd], lu_send.at[at, zd], lu_recv.at[at, zd], up)

    def l_down(group, k):
        at, zd = l_column(group), order[k]
        return remote(l_got.at[4 * group + k], l_high.at[at, zd], ld_send.at[at, zd], ld_recv.at[at, zd], down)

    def l_half_x():
        return remote(l_got.at[3, pl.ds(LIGHT_CUT, SMALL_HALF - LIGHT_CUT)], l_halves_x,
                      hx_send.at[items], hx_recv.at[items], x_side)

    def l_half_y():
        return remote(l_got.at[3, pl.ds(0, LIGHT_CUT)], l_halves_y, hy_send.at[items], hy_recv.at[items], y_side)

    def l_send_y():
        return remote(l_got.at[7], l_from_y, y_send.at[items], y_recv.at[items], y_side)

    def l_send_x():
        return remote(l_got.at[11], l_from_x, x_send.at[items], x_recv.at[items], x_side)

    leaving = (wide0, wide1, wide1, final)

    def pairs(section, micro):
        source = leaving[section]
        yield source.at[pl.ds(0, STUD_ROWS)], seg_stud.at[micro], seg_send.at[0, section], seg_recv.at[0, micro]
        yield source.at[pl.ds(STUD_ROWS, TEACH_END)], seg_teach.at[micro], seg_send.at[1, section], seg_recv.at[1, micro]
        yield stats.at[section], out_stats.at[micro], stat_send.at[section], stat_recv.at[micro]

    def exchange(section):
        return [remote(*pair, {"dp": me.dp, "pipe": section}) for pair in pairs(section, me.pipe)]

    def keep(section):
        return [pltpu.make_async_copy(src, dst, send) for src, dst, send, _ in pairs(section, me.pipe)]

    def arriving(micro):
        return [remote(*pair, {"dp": me.dp, "pipe": micro}) for pair in pairs(micro, micro)]

    for n in range(4 * items):
        share(*sequence[n]).start()
        if n == 5:
            for item in l_sequence:
                l_share(*item).start()
    for n in range(2):
        fetch(n).start()
    for group, k in l_sequence:
        l_fetch(group, k).start()
    row_copy = pltpu.make_async_copy(table.at[2 * x], owner_row, out_sem.at[2])
    row_copy.start()

    def bulk_item(n):
        group, k = sequence[n]
        at, slot = items * group + k, n % 4
        if n + 2 < 4 * items:
            fetch(n + 2).start()
        fetch(n).wait()
        share(group, k).wait_recv()
        if group == 0:
            add(got, at, stage, slot, 0, PART_ROWS, [])
            send_half_x(k).start()
            send_half_y(k).start()
        elif group == 1:
            send_half_x(k).wait_recv()
            add(got, at, stage, slot, 0, BACK_CUT, [])
            add(got, at, stage, slot, BACK_CUT, PART_ROWS - BACK_CUT, [(halves_x, k)])
            send_y(k).start()
        elif group == 2:
            send_half_y(k).wait_recv()
            add(got, at, stage, slot, 0, BACK_CUT, [(halves_y, k)])
            add(got, at, stage, slot, BACK_CUT, PART_ROWS - BACK_CUT, [])
            send_x(k).start()
        else:
            send_x(k).wait_recv()
            send_y(k).wait_recv()
            add(got, at, stage, slot, 0, PART_ROWS, [(from_x, k), (from_y, k)])

    def bulk_z(q):
        at, zd = 3 * items + q, order[q // PARTS]

        @pl.when(zd > z)
        def _():
            @pl.when(z > 0)
            def _():
                send_up(q).wait_recv()
                add(got, at, from_low, low_slot(q), 0, PART_ROWS, [])

            send_up(q).start()

        @pl.when(zd < z)
        def _():
            @pl.when(z < 3)
            def _():
                send_down(q).wait_recv()
                add(got, at, from_high, high_slot(q), 0, PART_ROWS, [])

            send_down(q).start()

    def light_item(group, k):
        at, zd, column = 4 * group + k, order[k], l_column(group)
        l_fetch(group, k).wait()
        l_share(group, k).wait_recv()
        add(l_got, at, l_stage, at, 0, SMALL_HALF, [])

        def merge(ref, slot):
            l_got[at] = (l_got[at].astype(FULL) + ref[column, slot].astype(FULL)).astype(LOW)

        if k < 3:

            @pl.when(zd > z)
            def _():
                @pl.when(z > 0)
                def _():
                    l_up(group, k).wait_recv()
                    merge(l_low, zd - 1)

                l_up(group, k).start()

            @pl.when(zd < z)
            def _():
                @pl.when(z < 3)
                def _():
                    l_down(group, k).wait_recv()
                    merge(l_high, zd)

                l_down(group, k).start()

        else:

            @pl.when(z > 0)
            def _():
                l_up(group, k).wait_recv()
                merge(l_low, zd - 1)

            @pl.when(z < 3)
            def _():
                l_down(group, k).wait_recv()
                merge(l_high, zd)

            if group == 0:
                l_half_x().start()
                l_half_y().start()

    def light_sides():
        l_half_x().wait_recv()
        l_got[7, LIGHT_CUT:SMALL_HALF, :] = (
            l_got[7, LIGHT_CUT:SMALL_HALF, :].astype(FULL) + l_halves_x[...].astype(FULL)
        ).astype(LOW)
        l_send_y().start()
        l_half_y().wait_recv()
        l_got[11, 0:LIGHT_CUT, :] = (
            l_got[11, 0:LIGHT_CUT, :].astype(FULL) + l_halves_y[...].astype(FULL)
        ).astype(LOW)
        l_send_x().start()

    def light_end():
        l_send_x().wait_recv()
        l_send_y().wait_recv()
        l_total[...] = l_got[15].astype(FULL) + l_from_x[...].astype(FULL) + l_from_y[...].astype(FULL)

    small_join = remote(late_half, late.at[pl.ds(0, SMALL_HALF)], join_send.at[0], join_recv.at[0], sibling)
    own_late = pltpu.make_async_copy(late, out_small.at[me.dp], out_sem.at[1])

    def late_z(origin, target, way):
        block = out_small.at[2 * origin + y]
        return remote(block, block, late_send.at[way, origin], late_recv.at[0, origin], target)

    def late_y(origin, yo):
        block = out_small.at[2 * origin + yo]
        return remote(block, block, late_send.at[2, origin], late_recv.at[1, origin], y_side)

    def late_step(k):
        @pl.when((core == 1) & (z >= k))
        def _():
            late_z(z - k, up, 0).wait_recv()
            pl.when(z < 3)(lambda: late_z(z - k, up, 0).start())
            late_y(z - k, y).start()

        @pl.when((core == 1) & (z + k <= 3))
        def _():
            late_z(z + k, down, 1).wait_recv()
            pl.when(z > 0)(lambda: late_z(z + k, down, 1).start())
            late_y(z + k, y).start()

    def leave():
        for section in range(4):
            @pl.when(me.pipe == section)
            def _(section=section):
                all_of(keep(section), lambda copy: copy.start())

            @pl.when(me.pipe != section)
            def _(section=section):
                all_of(exchange(section), lambda copy: copy.start())

    def late_start():
        light_end()

        @pl.when(core == 0)
        def _():
            late_half[...] = l_total[...].astype(LOW)
            small_join.start()

        @pl.when(core == 1)
        def _():
            late[SMALL_HALF:SMALL_ROWS, :] = l_total[...].astype(LOW)
            small_join.wait_recv()
            own_late.start()
            own_late.wait()
            pl.when(z < 3)(lambda: late_z(z, up, 0).start())
            pl.when(z > 0)(lambda: late_z(z, down, 1).start())
            late_y(z, y).start()

    def light_round(k):
        for n in range(4 * k, 4 * k + 4):
            light_item(*l_sequence[n])

    edge = (z == 0) | (z == 3)

    def early_z(k):
        pl.when(edge)(lambda: bulk_z(k))

    def inner_z(k):
        pl.when(jnp.logical_not(edge))(lambda: bulk_z(k))

    actions = {"LS": [light_sides], "LE": [late_start], "G": [leave]}
    numbered = {item: n for n, item in enumerate(sequence)}
    for k in range(4):
        actions["L%d" % k] = [functools.partial(light_round, k)]
        if k:
            actions["T%d" % k] = [functools.partial(late_step, k)]
    for q in range(items):
        for letter, group in (("A", 0), ("C", 1), ("B", 2), ("O", 3)):
            actions["%s%d" % (letter, q)] = [functools.partial(bulk_item, numbered[group, q])]
        if q < 3 * PARTS:
            actions["E%d" % q] = [functools.partial(early_z, q)]
            actions["I%d" % q] = [functools.partial(inner_z, q)]
    for event in REDUCE_ORDER:
        for action in actions[event]:
            action()

    row_copy.wait()
    part_sum[...] = jnp.sum((l_total[...] * l_total[...]).reshape(SMALL_HALF // 8, 8, 128), axis=0)
    lane = lax.broadcasted_iota(jnp.int32, (8, 128), 1)
    is_last = jnp.where((lane == me.dp) & (owner_row[...] == 7), 1.0, 0.0)
    weight = jnp.broadcast_to(jnp.sum(is_last, axis=1, keepdims=True), (8, 128))
    weight = jnp.where(core == 0, jnp.ones((8, 128), FULL), weight)

    big_parts = [pl.ds(PART_ROWS * n, PART_ROWS) for n in range(PARTS)]

    def big_join(n):
        return remote(total.at[big_parts[n]], out_big.at[1, big_parts[n]],
                      join_send.at[1 + n], join_recv.at[1 + n], sibling)

    def own_big(n):
        return pltpu.make_async_copy(total.at[big_parts[n]], out_big.at[0, big_parts[n]], big_sem.at[n])

    def end(n, low, high):
        q = 3 * PARTS + n

        def piece(begin, size, scale):
            part = pl.ds(begin, size)
            sums = got[3 * items + q, part, :].astype(FULL)
            if low:
                sums = sums + from_low[low_slot(q), part, :].astype(FULL)
            if high:
                sums = sums + from_high[high_slot(q), part, :].astype(FULL)
            total[pl.ds(PART_ROWS * n + begin, size), :] = sums
            squares = jnp.sum((sums * sums).reshape(size // 8, 8, 128), axis=0)
            part_sum[...] += squares if scale is None else squares * scale

        def plain(begin, size):
            piece(begin, size, None)

        if n < PARTS - 1:
            over(0, PART_ROWS, plain)
        else:
            over(0, PART_ROWS - EDGE, plain)
            piece(PART_ROWS - EDGE, EDGE, weight)

    for n in range(PARTS):
        q = 3 * PARTS + n

        @pl.when(z == 0)
        def _(n=n, q=q):
            send_down(q).wait_recv()
            end(n, False, True)

        @pl.when((z > 0) & (z < 3))
        def _(n=n, q=q):
            send_up(q).wait_recv()
            send_down(q).wait_recv()
            end(n, True, True)

        @pl.when(z == 3)
        def _(n=n, q=q):
            send_up(q).wait_recv()
            end(n, True, False)

        @pl.when(core == 0)
        def _(n=n):
            own_big(n).start()

        @pl.when(core == 1)
        def _(n=n):
            big_join(n).start()

    def along_pipe(step, slot):
        target = {"dp": me.dp, "pipe": lax.rem(me.pipe + step, 4)}
        return remote(part_sum, by_pipe.at[slot], p_send.at[step], p_recv.at[step], target)

    def along_dp(step, slot):
        target = {"dp": lax.rem(me.dp + step, 8), "pipe": me.pipe}
        return remote(mine, by_dp.at[slot], d_send.at[step], d_recv.at[step], target)

    for step in range(1, 4):
        along_pipe(step, me.pipe).start()
    by_pipe[me.pipe] = part_sum[...]
    for step in range(1, 4):
        along_pipe(step, lax.rem(me.pipe + 4 - step, 4)).wait_recv()
    mine[...] = jnp.sum(by_pipe[...], axis=0)
    for step in range(1, 8):
        along_dp(step, me.dp).start()
    by_dp[me.dp] = mine[...]
    for step in range(1, 8):
        along_dp(step, lax.rem(me.dp + 8 - step, 8)).wait_recv()
    whole = jnp.sum(jnp.sum(by_dp[...], axis=0), axis=0, keepdims=True)
    length = jnp.sqrt(jnp.broadcast_to(jnp.sum(whole, axis=1, keepdims=True), (8, 128)))
    norm[...] = length
    factor[...] = jnp.minimum(1.0, CLIP_NORM / length)

    @pl.when(core == 0)
    def _():
        for n in range(PARTS):
            own_big(n).wait()
            big_join(n).wait_recv()
        small_join.wait_send()

    @pl.when(core == 1)
    def _():
        for n in range(PARTS):
            big_join(n).wait_send()
        for origin in range(4):
            late_y(origin, 1 - y).wait_recv()
            late_y(origin, y).wait_send()
            pl.when((z < 3) & (origin <= z))(lambda: late_z(origin, up, 0).wait_send())
            pl.when((z > 0) & (origin >= z))(lambda: late_z(origin, down, 1).wait_send())

    for other in range(4):
        @pl.when(me.pipe == other)
        def _(other=other):
            all_of(keep(other), lambda copy: copy.wait())

        @pl.when(me.pipe != other)
        def _(other=other):
            all_of(exchange(other), lambda copy: copy.wait_send())
            all_of(arriving(other), lambda copy: copy.wait_recv())

    for step in range(1, 4):
        along_pipe(step, me.pipe).wait_send()
    for step in range(1, 8):
        along_dp(step, me.dp).wait_send()
    for copy in (l_half_x(), l_half_y(), l_send_x(), l_send_y()):
        copy.wait_send()
    for q in range(items):
        send_half_x(q).wait_send()
        send_half_y(q).wait_send()
        send_x(q).wait_send()
        send_y(q).wait_send()
        for group in range(4):
            share(group, q).wait_send()
    for group, k in l_sequence:
        l_share(group, k).wait_send()
    for k in range(3):
        zd = order[k]

        @pl.when(zd > z)
        def _(k=k):
            for n in range(PARTS):
                send_up(PARTS * k + n).wait_send()
            for group in range(4):
                l_up(group, k).wait_send()

        @pl.when(zd < z)
        def _(k=k):
            for n in range(PARTS):
                send_down(PARTS * k + n).wait_send()
            for group in range(4):
                l_down(group, k).wait_send()


def reduce_all(big, small, wide0, wide1, final, stats, table):
    sem = pltpu.SemaphoreType.DMA
    vm = pltpu.VMEM
    items = 4 * PARTS
    lane_tile = jax.ShapeDtypeStruct((8, 128), FULL)
    return pl.pallas_call(
        reduce_kernel,
        name="reduce_all",
        out_shape=(
            jax.ShapeDtypeStruct((2, BIG_HALF, 128), FULL),
            jax.ShapeDtypeStruct((8, SMALL_ROWS, 128), LOW),
            jax.ShapeDtypeStruct((4, STUD_ROWS, C_OUT), LOW),
            jax.ShapeDtypeStruct((4, TEACH_END, C_OUT), LOW),
            jax.ShapeDtypeStruct((4,) + stats.shape[1:], FULL),
            lane_tile,
            lane_tile,
        ),
        in_specs=[any_spec()] * 7,
        out_specs=(any_spec(),) * 5 + (vmem_spec(),) * 2,
        scratch_shapes=[
            vm((4 * items, PART_ROWS, 128), LOW),
            vm((items, PART_ROWS - BACK_CUT, 128), LOW), vm((items, BACK_CUT, 128), LOW),
            vm((items, PART_ROWS, 128), LOW), vm((items, PART_ROWS, 128), LOW),
            vm((3 * PARTS, PART_ROWS, 128), LOW), vm((3 * PARTS, PART_ROWS, 128), LOW),
            vm((4, PART_ROWS, 128), LOW), vm((BIG_HALF, 128), FULL),
            vm((16, SMALL_HALF, 128), LOW), vm((16, SMALL_HALF, 128), LOW),
            vm((4, 3, SMALL_HALF, 128), LOW), vm((4, 3, SMALL_HALF, 128), LOW),
            vm((SMALL_HALF - LIGHT_CUT, 128), LOW), vm((LIGHT_CUT, 128), LOW),
            vm((SMALL_HALF, 128), LOW), vm((SMALL_HALF, 128), LOW), vm((SMALL_HALF, 128), FULL),
            vm((SMALL_ROWS, 128), LOW), vm((SMALL_HALF, 128), LOW), vm((8, 128), jnp.int32),
            vm((4, 8, 128), FULL), vm((8, 8, 128), FULL), vm((8, 128), FULL), vm((8, 128), FULL),
            sem((4 * items,)), sem((4 * items,)), sem((16,)), sem((16,)),
            sem((items + 1,)), sem((items + 1,)), sem((items + 1,)), sem((items + 1,)),
            sem((items + 1,)), sem((items + 1,)), sem((items + 1,)), sem((items + 1,)),
            sem((3 * PARTS,)), sem((3 * PARTS,)), sem((3 * PARTS,)), sem((3 * PARTS,)),
            sem((4, 3)), sem((4, 3)), sem((4, 3)), sem((4, 3)),
            sem((4,)), sem((16,)), sem((3,)), sem((PARTS,)), sem((3, 4)), sem((2, 4)),
            sem((1 + PARTS,)), sem((1 + PARTS,)),
            sem((2, 4)), sem((2, 4)), sem((4,)), sem((4,)), sem((4,)), sem((4,)), sem((8,)), sem((8,)),
        ],
        compiler_params=pltpu.CompilerParams(
            collective_id=1, has_side_effects=True, vmem_limit_bytes=62 << 20
        ),
    )(big.reshape(2, 8, 2, BIG_HALF, 128), small.reshape(2, 8, 2, SMALL_HALF, 128),
      wide0, wide1, final, stats, table)


def high_dot(a, b, dims=((1,), (0,))):
    return lax.dot_general(a, b, (dims, ((), ())), precision=HIGH, preferred_element_type=FULL)


PIECES = 7
FRONT = 48


def update_kernel(owners, factor_ref, norm, big, small, gram_old, basis_old, params, moment, second,
                  clipped, moment_new, second_new, params_new, gram_new, basis_new, length,
                  tiles, low, grad, held, rotated, weights, gram, in_sem, out_sem, tile_sem):
    factor = factor_ref[0:1, :]
    length[0, 0] = jnp.max(norm[...])
    block, section = owners[0, lax.axis_index("dp")], lax.axis_index("pipe")
    even = lax.rem(section, 2) == 0
    span = params.shape[0]
    piece = held.shape[0] // PIECES

    quarter = WINDOW // 4 * TILE

    def big_load(i):
        part = pl.ds(quarter * i, min(quarter, BIG_ROWS - quarter * i))
        return pltpu.make_async_copy(big.at[part], tiles.at[part], tile_sem.at[i])

    @pl.when(even)
    def _():
        for i in range(4):
            big_load(i).start()

    def loads(i):
        part = pl.ds(piece * i, min(piece, span - piece * i))
        for n, (src, dst) in enumerate(((params, weights), (moment, held), (second, rotated))):
            yield pltpu.make_async_copy(src.at[part, 0, :], dst.at[part], in_sem.at[n, i])

    def stores(i):
        count = min(piece, span - piece * i)
        part = pl.ds(piece * i, count)
        yield pltpu.make_async_copy(
            grad.at[pl.ds(FRONT + piece * i, count)], clipped.at[part, 0, :], out_sem.at[3, i])
        pairs = ((held, moment_new), (rotated, second_new), (weights, params_new))
        for n, (src, dst) in enumerate(pairs):
            yield pltpu.make_async_copy(src.at[part], dst.at[part, 0, :], out_sem.at[n, i])

    for i in range(PIECES):
        for load in loads(i):
            load.start()

    @pl.when(jnp.logical_not(even))
    def _():
        low[...] = jnp.zeros_like(low)

        @pl.when(block == 0)
        def _():
            copy = pltpu.make_async_copy(small.at[0:20], low, tile_sem.at[0])
            copy.start()
            copy.wait()

        @pl.when(block == 1)
        def _():
            copy = pltpu.make_async_copy(small.at[19:33], low.at[0:14], tile_sem.at[0])
            copy.start()
            copy.wait()

        @pl.loop(0, WINDOW)
        def _(r):
            tiles[pl.ds(pl.multiple_of(TILE * r, TILE), TILE), :] = low[r].astype(FULL)

    def lay_flat(r):
        narrow, plain = tile_forms(section, STRIDE * block + r)
        edge = even & (r == STRIDE)
        narrow, plain = narrow & jnp.logical_not(edge), plain | edge
        base = FRONT - 6 * block + TILE * r
        here = pl.multiple_of(TILE * r, TILE)

        @pl.when(narrow)
        def _():
            for j in range(4):
                grad[pl.ds(base + j, 64, 4), :] = tiles[pl.ds(here + 64 * j, 64), :]

        @pl.when(plain)
        def _():
            grad[pl.ds(base, TILE), :] = tiles[pl.ds(here, TILE), :]

        @pl.when(jnp.logical_not(narrow | plain))
        def _():
            for j in range(16):
                grad[pl.ds(base + j, 16, 16), :] = tiles[pl.ds(here + 16 * j, 16), :]

    for i in range(4):
        pl.when(even)(lambda: big_load(i).wait())
        pl.loop(WINDOW // 4 * i, WINDOW // 4 * (i + 1))(lay_flat)

    tail = piece * PIECES - 8
    rest = lax.broadcasted_iota(jnp.int32, (8, 128), 0) + tail
    grad[FRONT + tail : FRONT + tail + 8, :] = jnp.where(
        rest < span, grad[FRONT + tail : FRONT + tail + 8, :], 0.0
    )
    gram[...] = jnp.zeros_like(gram)

    def halves(value):
        high = value.astype(LOW)
        return high, (value - high.astype(FULL)).astype(LOW)

    def split_dot(a, b, dims=((1,), (0,))):
        def dot(left, right):
            return lax.dot_general(left, right, (dims, ((), ())), preferred_element_type=FULL)

        return dot(a[0], b[0]) + (dot(a[0], b[1]) + dot(a[1], b[0]))

    @pl.loop(0, PIECES)
    def _(i):
        part = halves(grad[pl.ds(pl.multiple_of(FRONT + piece * i, 8), piece), :])
        gram[...] += split_dot(part, part, ((0,), (0,)))

    old = basis_old[...]
    fresh = DECAY_STATS * gram_old[...] + (1.0 - DECAY_STATS) * (gram[...] * (factor * factor))
    gram_new[...] = fresh
    product = high_dot(fresh, old)
    rotation = product / jnp.sqrt(jnp.sum(product * product))
    for repeat in range(NS_STEPS):
        parts = halves(rotation)
        square = split_dot(parts, parts, ((0,), (0,)))
        rotation = 1.5 * rotation - 0.5 * split_dot(parts, halves(square))
    basis_new[...] = rotation
    change = halves(high_dot(old, rotation, ((0,), (0,))))
    turn = halves(rotation)
    correction = math.sqrt(1.0 - DECAY_SECOND**STEP) / (1.0 - DECAY_FIRST**STEP)
    for i in range(PIECES):
        for load in loads(i):
            load.wait()
        at = slice(FRONT + piece * i, FRONT + piece * i + piece)
        part = slice(piece * i, piece * i + piece)
        clip = grad[at, :] * factor
        grad[at, :] = clip
        turned = split_dot(halves(clip), turn)
        first = DECAY_FIRST * split_dot(halves(held[part, :]), change) + (1.0 - DECAY_FIRST) * turned
        power = DECAY_SECOND * rotated[part, :] + (1.0 - DECAY_SECOND) * turned * turned
        held[part, :] = first
        rotated[part, :] = power
        scaled = halves(first / (jnp.sqrt(power) + ADAM_EPS))
        direction = split_dot(scaled, turn, ((1,), (1,))) * correction
        before = weights[part, :]
        weights[part, :] = before - LEARN_RATE * (direction + WEIGHT_DECAY * before)
        for store in stores(i):
            store.start()
    for i in range(PIECES):
        for store in stores(i):
            store.wait()


def update(owners, factor, norm, big, small, gram_old, basis_old, params, moment, second):
    span = params.shape[1] // 128
    rows = -(-span // (8 * PIECES)) * 8 * PIECES
    flat_shape = jax.ShapeDtypeStruct((span, 1, 128), FULL)
    square = jax.ShapeDtypeStruct((128, 128), FULL)
    sem = pltpu.SemaphoreType.DMA
    vm = pltpu.VMEM
    outs = pl.pallas_call(
        update_kernel,
        name="update",
        out_shape=(flat_shape,) * 4 + (square,) * 2 + (jax.ShapeDtypeStruct((1, 1), FULL),),
        in_specs=[smem_spec()] + [vmem_spec()] * 2 + [any_spec()] * 2 + [vmem_spec()] * 2 + [any_spec()] * 3,
        out_specs=(any_spec(),) * 4 + (vmem_spec(),) * 2 + (smem_spec(),),
        scratch_shapes=[
            vm((WINDOW * TILE, 128), FULL), vm((WINDOW, TILE, 128), LOW),
            vm((FRONT + WINDOW * TILE, 128), FULL), vm((rows, 128), FULL), vm((rows, 128), FULL),
            vm((rows, 128), FULL), vm((128, 128), FULL), sem((3, PIECES)), sem((4, PIECES)), sem((4,)),
        ],
        compiler_params=pltpu.CompilerParams(vmem_limit_bytes=60 << 20),
    )(owners, factor, norm, big.reshape(BIG_ROWS, 128), small.reshape(USED_TILES[1], TILE, 128),
      gram_old, basis_old, params.reshape(span, 1, 128), moment.reshape(span, 1, 128),
      second.reshape(span, 1, 128))
    return tuple(out.reshape(1, span * 128) for out in outs[:4]) + outs[4:]


def to_phases(teach, stud):
    def split(part, axes):
        crops, high, across, channels = part.shape
        part = part.reshape(crops, high // 2, 2, across // 2, 2, channels).transpose(axes)
        return part.reshape(4, -1, channels)

    zeros = jnp.zeros((4, PADDED - ROWS, teach.shape[-1]), teach.dtype)
    parts = [split(stud, (2, 4, 0, 1, 3, 5)), split(teach, (2, 4, 1, 3, 0, 5)), zeros]
    return jnp.concatenate(parts, axis=1)


def from_phases(phases, shape, crops_last):
    crops, high, across, channels = shape
    if crops_last:
        part = phases.reshape(2, 2, high // 2, across // 2, crops, channels).transpose(4, 2, 0, 3, 1, 5)
    else:
        part = phases.reshape(2, 2, crops, high // 2, across // 2, channels).transpose(2, 3, 0, 4, 1, 5)
    return part.reshape(shape)


def on_small_slice(
    teach_in,
    stud_in,
    params,
    owners,
    depth_gates,
    teach_ids,
    stud_ids,
    targets,
    moment,
    second,
    gram_stats,
    eigen_basis,
):
    phases = to_phases(teach_in[0], stud_in[0])
    big, small, ids = prepare(owners, params)
    all_big, all_small, table = gather_all(big, small, ids)
    wide_0, wide_1, final, stats, grad_x, out_big, out_small = run_step(
        table,
        depth_gates,
        teach_ids.T,
        stud_ids,
        all_big.reshape(2, 8, BIG_ROWS, 128),
        all_small.reshape(2, USED_TILES[1], TILE, 128),
        phases,
        targets,
    )
    sum_big, sum_small, segment_stud, segment_teach, stats, norm, factor = reduce_all(
        out_big, out_small, wide_0, wide_1, final, stats, table
    )
    clipped, moment_new, second_new, params_new, gram_new, rotation, length = update(
        owners, factor, norm, sum_big, sum_small, gram_stats[0], eigen_basis[0], params, moment, second
    )
    teach_shape, stud_shape = teach_in.shape[1:], stud_in.shape[1:]
    small_teach = (teach_shape[1] // 2, teach_shape[2] // 2, teach_shape[0], C_OUT)
    small_stud = (stud_shape[0], stud_shape[1] // 2, stud_shape[2] // 2, C_OUT)
    segment_teach = segment_teach[:, : ROWS - STUD_ROWS].reshape((4,) + small_teach).transpose(0, 3, 1, 2, 4)
    segment_stud = segment_stud.reshape((4,) + small_stud)
    stats = stats[:, 0:2]
    teach_grad = from_phases(grad_x[:, STUD_ROWS:ROWS], teach_shape, True)
    stud_grad = from_phases(grad_x[:, :STUD_ROWS], stud_shape, False)
    grad_norm = length.reshape(())
    return (
        segment_teach[None],
        segment_stud[None],
        teach_grad[None],
        stud_grad[None],
        stats[None, :, None],
        grad_norm,
        clipped,
        moment_new,
        second_new,
        params_new,
        gram_new[None],
        rotation[None],
    )


def solution(mesh):
    placed = (
        P("pipe", "dp", None, None, None),
        P("pipe", "dp", None, None, None),
        P("pipe", "dp"),
        P("pipe", None),
        P(),
        P(None, "dp"),
        P(None, "dp"),
        P(),
        P("pipe", "dp"),
        P("pipe", "dp"),
        P("pipe", "dp", None),
        P("pipe", "dp", None),
    )
    small_slice = mesh.shape["dp"] == 8 and mesh.shape["pipe"] == 4
    return jax.shard_map(
        on_small_slice if small_slice else on_device,
        mesh=mesh,
        in_specs=placed,
        out_specs=(
            P("pipe", None, "dp", None, None, None),
            P("pipe", None, "dp", None, None, None),
            P("pipe", "dp", None, None, None),
            P("pipe", "dp", None, None, None),
            P("pipe", None, "dp", None, None),
            P(),
            P("pipe", "dp"),
            P("pipe", "dp"),
            P("pipe", "dp"),
            P("pipe", "dp"),
            P("pipe", "dp", None),
            P("pipe", "dp", None),
        ),
        check_vma=False,
    )
```

profile of v0, /device:TPU:0, one launch (start us, length us, event | category | flops | bytes accessed | tf_op | source)
XLA Modules:
  0.0 304.2 jit_solution(16558924514908771383)
XLA Ops:
  0.6 0.0 copy-start.2
  0.7 0.1 pad.2.clone
  0.7 1.2 reshape_squeeze.6
  1.9 0.2 copy.33
  2.1 0.1 reshape.89
  2.2 0.0 copy-done.2
  2.2 0.4 copy.32
  2.7 0.2 reshape.90
  2.9 1.3 maximum_maximum_fusion.x
  4.2 4.7 %prepare.1 = (bf16[4928,128]{1,0:T(8,128)(2,1)}, bf16[33,256,128]{2,1,0:T(8,128)(2,1)}, s32[8,128]{1,0:T(8,128)}) custom-call(s32[1,8]{1,0:T(1,128)} %owners.3, f32[4870,1,128]{2,1,0:T(1,128)} %bitcast.41), custom_call_target="tpu_custom_call" | custom-call | tf_op jit(solution)/shard_map/prepare/pallas_call | solution.py:570
  9.0 109.3 %gather_all.1 = (bf16[2,8,2,2464,128]{4,3,2,1,0:T(8,128)(2,1)}, bf16[2,8,2,528,128]{4,3,2,1,0:T(8,128)(2,1)}, s32[4,8,128]{2,1,0:T(8,128)}) custom-call(bf16[4928,128]{1,0:T(8,128)(2,1)} %get-tuple-element.39.big, bf16[8,1056,128]{2,1,0:T(8,128)(2,1)} %bitcast.51, s32[8,128]{1,0:T(8,128)} %get-tuple-element.41.ids), custom_call_target="tpu_custom_call" | custom-call | tf_op jit(solution)/shard_map/gather_all/pallas_call | solution.py:990
  118.3 35.8 %step.1 = (bf16[128,2048]{1,0:T(8,128)(2,1)}, bf16[128,2048]{1,0:T(8,128)(2,1)}, bf16[128,2048]{1,0:T(8,128)(2,1)}, f32[4,8,3072]{2,1,0:T(8,128)}, bf16[4,128,10...) custom-call(s32[4,8,128]{2,1,0:T(8,128)} %get-tuple-element.42.table, ...), custom_call_target="tpu_custom_call" | custom-call | tf_op jit(solution)/shard_map/step/pallas_call | solution.py:1491
  154.2 122.8 %reduce_all.1 = (f32[2,2464,128]{2,1,0:T(8,128)}, bf16[8,1056,128]{2,1,0:T(8,128)(2,1)}, bf16[4,48,2048]{2,1,0:T(8,128)(2,1)}, bf16[4,80,2048]{2,1,0:T(8,128)(2,...) custom-call(bf16[2,8,2,2464,128]{4,3,2,1,0:T(8,128)(2,1)} %bitcast.39, ...), custom_call_target="tpu_custom_call" | custom-call | tf_op jit(solution)/shard_map/reduce_all/pallas_call | solution.py:2023
  277.0 0.0 copy-start
  277.0 1.4 slice.12
  278.4 1.6 reshape.93
  280.0 1.7 slice_bitcast_fusion
  281.7 0.0 copy-done
  281.8 0.0 copy-start.1
  281.8 0.2 reshape.94
  282.0 1.3 copy.27
  283.3 0.1 reshape.95
  283.5 0.4 copy.28
  283.9 0.9 broadcast_in_dim_reshape.11
  284.8 0.0 copy-done.1
  284.8 1.2 broadcast_in_dim_reshape.9
  286.0 18.0 %update.1 = (f32[4870,1,128]{2,1,0:T(1,128)}, f32[4870,1,128]{2,1,0:T(1,128)}, f32[4870,1,128]{2,1,0:T(1,128)}, f32[4870,1,128]{2,1,0:T(1,128)}, f32[128,128]{1,...) custom-call(s32[1,8]{1,0:T(1,128)} %owners.3, f32[8,128]{1,0:T(8,128)} %get-tuple-element.55.factor_ref, ...), custom_call_target="tpu_custom_call" | custom-call | tf_op jit(solution)/shard_map/update/pallas_call | solution.py:2222
  (3 shorter events, 0.1 us)
Async XLA Ops:
  0.6 1.6 copy-start.2
  277.0 4.7 %copy-start = (bf16[4,128,1024]{2,1,0:T(8,128)(2,1)S(1)}, bf16[4,128,1024]{2,1,0:T(8,128)(2,1)}, u32[]{:S(2)}) copy-start(bf16[4,128,1024]{2,1,0:T(8,128)(2,1)} %get-tuple-element.53) | copy-start | bytes 3145732
  281.8 3.1 %copy-start.1 = (bf16[4,48,2048]{2,1,0:T(8,128)(2,1)S(1)}, bf16[4,48,2048]{2,1,0:T(8,128)(2,1)}, u32[]{:S(2)}) copy-start(bf16[4,48,2048]{2,1,0:T(8,128)(2,1)} %get-tuple-element.52) | copy-start | bytes 2359300
where the time goes:
time: 307 us; the launch traced here: 304 us
  Pallas kernels  291 us (95%)
  local copies, waits for them, and re-layouts  11.2 us (4%)
    pallas_call x1, Pallas kernels, reduce_all(): pl.pallas_call(reduce_kernel, name='reduce_all', out_shape=(jax.ShapeDtyp...  123 us
    pallas_call x1, Pallas kernels, gather_all(): pl.pallas_call(gather_kernel, name='gather_all', out_shape=(jax.ShapeDtyp...  109 us
    pallas_call x1, Pallas kernels, run_step(): pl.pallas_call(step_kernel, name='step', out_shape=(wide, wide, wide, jax...  35.8 us
    pallas_call x1, Pallas kernels, update(): pl.pallas_call(update_kernel, name='update', out_shape=(flat_shape,) * 4...  18 us

commit v1 on v0

--- a/solution.py
+++ b/solution.py
@@ -623,18 +623,18 @@
 PART_ROWS = BIG_HALF // PARTS
 BULK_CUT = 480
 LIGHT_CUT = 256
-BACK_CUT = 720
+BACK_CUT = 768
 GATHER_ORDER = (
-    "X1", "Z2", "EY", "EC0", "Z3", "Y0", "X2", "EC1", "X3", "Y1", "Y2", "R0", "EC2", "R1", "EC3",
-    "Y3", "Z4", "L0", "X4", "Z5", "L1", "S0", "X5", "Y4", "R2", "S1", "L2", "S2", "Y5", "Z6", "R3",
-    "Y6", "X6", "S3", "Z7", "Y7", "M1", "S4", "S5", "D0", "D1", "X7", "R4", "S6", "M2", "D2", "S7",
-    "D3", "R5", "R6", "R7", "M3", "D4", "D5", "D6", "D7",
+    "X1", "Z2", "X2", "Y0", "EY", "EC0", "EC1", "R0", "Z3", "Y1", "Z4", "Y2", "X3", "EC2", "R1",
+    "EC3", "Y3", "L0", "X4", "Z5", "L1", "Z6", "X5", "S0", "S1", "R2", "Y4", "Y5", "S2", "L2",
+    "Y6", "R3", "Z7", "X6", "Y7", "M1", "S3", "S4", "R4", "X7", "D0", "D1", "S5", "S6", "R5", "M2",
+    "R6", "D2", "S7", "D3", "R7", "D4", "D5", "M3", "D6", "D7",
 )
 REDUCE_ORDER = (
-    "A0", "A1", "A2", "A3", "A4", "A5", "L0", "A6", "C0", "B0", "C1", "B1", "C2", "L1", "B2", "B3",
-    "L2", "L3", "A7", "C3", "O0", "LS", "B4", "C4", "O1", "E0", "C5", "O2", "E1", "B5", "LE", "I0",
-    "I1", "B6", "T1", "I2", "C6", "C7", "B7", "E2", "G", "O3", "O4", "I3", "I4", "O5", "T2", "I5",
-    "E3", "E4", "E5", "T3", "O6", "O7",
+    "A0", "A1", "A2", "A3", "A4", "A5", "L0", "B0", "C0", "C1", "B1", "B2", "B3", "C2", "L1", "L2",
+    "A6", "L3", "B4", "C3", "O0", "LS", "A7", "O1", "B5", "B6", "E0", "C4", "O2", "O3", "E1", "E2",
+    "C5", "C6", "I0", "B7", "LE", "C7", "I1", "E3", "T1", "I2", "I3", "O4", "O5", "G", "T2", "E4",
+    "I4", "O6", "I5", "E5", "O7", "T3",
 )
 
 
@@ -1097,8 +1097,10 @@
     return run
 
 
-def step_kernel(table, gates, teach_ids, stud_ids, all_big, all_small, x, targets, grid,
-                wide0, wide1, final, stats, grad_x, out_big, out_small,
+def step_kernel(table, gates, teach_ids, stud_ids, all_big, all_small, teach_x, stud_x, targets, grid,
+                moves,
+                wide0, wide1, final, stats, grad_teach, grad_stud, out_big, out_small,
+                x,
                 w0, w1, w2, w3, edges, loose, vec, grad_vec, raw,
                 std_a, std_b, std_p, std_1, std_c, std_d, hidden, cols0, cols2,
                 nar0, nar2, turned, turned_x, relay, dz_a, dz_n, acc, acc_x, grad_h,
@@ -1225,6 +1227,16 @@
                 phase = 2 * (1 if r != 1 else 0) + (1 if q != 1 else 0)
                 yield t, phase, -1 if r == 0 else 0, -1 if q == 0 else 0
 
+    def one_hot(index, width):
+        lane = lax.broadcasted_iota(jnp.int32, index.shape, 1)
+        parts = [jnp.where(lane + start == index, 1.0, 0.0) for start in range(0, width, 128)]
+        return jnp.concatenate(parts, axis=1)[:, 0:width].astype(LOW)
+
+    for p in range(4):
+        at = slice(PADDED * p, PADDED * p + PADDED)
+        from_teach = mul(one_hot(moves[0, at, :], teach_x.shape[0]), teach_x[...])
+        x[p] = (from_teach + mul(one_hot(moves[1, at, :], stud_x.shape[0]), stud_x[...])).astype(LOW)
+
     settle(0, (0, 7))
     whole_x = x[...].reshape(4 * PADDED, C_IN)
     for c in range(2):
@@ -1459,14 +1471,17 @@
         for p in range(4):
             dz_a[PADDED * p : PADDED * p + PADDED, at] = pad_low(result[ROWS * p : ROWS * p + ROWS])
 
+    place_teach = one_hot(moves[2, 0 : teach_x.shape[0], :], 4 * PADDED)
+    place_stud = one_hot(moves[3, 0 : stud_x.shape[0], :], 4 * PADDED)
+
     @chunks(4)
     def _(c):
         at = lanes(c)
         low = dz_a[...]
         part = mul_t(low, narrow_part(w0, 4 * c, 4))
-        grad_x[0, :, at] = (part[0:PADDED] + acc_x[:, at]).astype(LOW)
-        for p in range(1, 4):
-            grad_x[p, :, at] = part[PADDED * p : PADDED * p + PADDED].astype(LOW)
+        part = jnp.concatenate([part[0:PADDED] + acc_x[:, at], part[PADDED:]], axis=0).astype(LOW)
+        grad_teach[:, at] = mul(place_teach, part).astype(LOW)
+        grad_stud[:, at] = mul(place_stud, part).astype(LOW)
         put_narrow(w0, 4 * c, 4, mul(x[:, :, at].reshape(4 * PADDED, 256).T, low))
 
     flush(0)
@@ -1479,12 +1494,21 @@
         store.wait()
 
 
-def run_step(table, gates, teach_ids, stud_ids, all_big, all_small, phases, targets):
+def run_step(table, gates, teach_ids, stud_ids, all_big, all_small, teach_x, stud_x, targets):
     spots = np.zeros((3, ROWS, 128), np.int32)
     for r in range(ROWS):
         width = 4 if r < STUD_ROWS else 6
         at = r % 16 if r < STUD_ROWS else (r - STUD_ROWS) // 2
         spots[0, r], spots[1, r], spots[2, r] = at // width, at % width, width
+    moves = np.full((4, 4 * PADDED, 128), -1, np.int32)
+    for p in range(4):
+        for r in range(ROWS):
+            high, across = 2 * spots[0, r, 0] + p // 2, 2 * spots[1, r, 0] + p % 2
+            group, lies = 1, 64 * (r // 16) + 8 * high + across
+            if r >= STUD_ROWS:
+                group, lies = 0, 2 * (12 * high + across) + (r - STUD_ROWS) % 2
+            moves[group, PADDED * p + r] = lies
+            moves[2 + group, lies] = PADDED * p + r
     sem = pltpu.SemaphoreType.DMA
     wide = jax.ShapeDtypeStruct((PADDED, C_OUT), LOW)
     vm = pltpu.VMEM
@@ -1494,13 +1518,15 @@
         out_shape=(
             wide, wide, wide,
             jax.ShapeDtypeStruct((4, 8, 2 * MID + C_OUT), FULL),
-            jax.ShapeDtypeStruct((4, PADDED, C_IN), LOW),
+            jax.ShapeDtypeStruct(teach_x.shape, LOW),
+            jax.ShapeDtypeStruct(stud_x.shape, LOW),
             jax.ShapeDtypeStruct((2, 8, BIG_ROWS, 128), LOW),
             jax.ShapeDtypeStruct((2, USED_TILES[1], TILE, 128), LOW),
         ),
-        in_specs=[smem_spec()] * 4 + [any_spec(), any_spec(), vmem_spec(), any_spec(), vmem_spec()],
-        out_specs=(vmem_spec(),) * 5 + (any_spec(),) * 2,
+        in_specs=[smem_spec()] * 4 + [any_spec()] * 2 + [vmem_spec()] * 2 + [any_spec()] + [vmem_spec()] * 2,
+        out_specs=(vmem_spec(),) * 6 + (any_spec(),) * 2,
         scratch_shapes=[
+            vm((4, PADDED, C_IN), LOW),
             vm((153, TILE, 128), LOW), vm((33, TILE, 128), LOW), vm((115, TILE, 128), LOW), vm((33, TILE, 128), LOW),
             vm((13, EDGE, 128), LOW), vm((TILE, 128), FULL), vm((4, 48, 128), FULL), vm((4, TILE, 128), FULL),
             vm((8, 2 * MID + C_OUT), FULL),
@@ -1514,7 +1540,7 @@
             sem((2, 16)), sem((18,)), sem((36,)),
         ],
         compiler_params=pltpu.CompilerParams(vmem_limit_bytes=60 << 20),
-    )(table, gates, teach_ids, stud_ids, all_big, all_small, phases, targets, jnp.asarray(spots))
+    )(table, gates, teach_ids, stud_ids, all_big, all_small, teach_x, stud_x, targets, jnp.asarray(spots), jnp.asarray(moves))
 
 
 def reduce_kernel(big, small, wide0, wide1, final, stats, table,
@@ -2070,9 +2096,9 @@
 FRONT = 48
 
 
-def update_kernel(owners, factor_ref, norm, big, small, gram_old, basis_old, params, moment, second,
-                  clipped, moment_new, second_new, params_new, gram_new, basis_new, length,
-                  tiles, low, grad, held, rotated, weights, gram, in_sem, out_sem, tile_sem):
+def update_kernel(owners, factor_ref, norm, big, small, gram_old, basis_old, params, moment, second, stats,
+                  clipped, moment_new, second_new, params_new, gram_new, basis_new, length, out_stats,
+                  tiles, low, grad, held, rotated, weights, gram, in_sem, out_sem, tile_sem, stat_sem):
     factor = factor_ref[0:1, :]
     length[0, 0] = jnp.max(norm[...])
     block, section = owners[0, lax.axis_index("dp")], lax.axis_index("pipe")
@@ -2080,6 +2106,12 @@
     span = params.shape[0]
     piece = held.shape[0] // PIECES
 
+    stat_copies = [
+        pltpu.make_async_copy(stats.at[m, pl.ds(0, 2)], out_stats.at[m], stat_sem.at[m])
+        for m in range(stats.shape[0])
+    ]
+    for copy in stat_copies:
+        copy.start()
     quarter = WINDOW // 4 * TILE
 
     def big_load(i):
@@ -2210,9 +2242,11 @@
     for i in range(PIECES):
         for store in stores(i):
             store.wait()
-
-
-def update(owners, factor, norm, big, small, gram_old, basis_old, params, moment, second):
+    for copy in stat_copies:
+        copy.wait()
+
+
+def update(owners, factor, norm, big, small, gram_old, basis_old, params, moment, second, stats):
     span = params.shape[1] // 128
     rows = -(-span // (8 * PIECES)) * 8 * PIECES
     flat_shape = jax.ShapeDtypeStruct((span, 1, 128), FULL)
@@ -2222,39 +2256,19 @@
     outs = pl.pallas_call(
         update_kernel,
         name="update",
-        out_shape=(flat_shape,) * 4 + (square,) * 2 + (jax.ShapeDtypeStruct((1, 1), FULL),),
-        in_specs=[smem_spec()] + [vmem_spec()] * 2 + [any_spec()] * 2 + [vmem_spec()] * 2 + [any_spec()] * 3,
-        out_specs=(any_spec(),) * 4 + (vmem_spec(),) * 2 + (smem_spec(),),
+        out_shape=(flat_shape,) * 4 + (square,) * 2 + (jax.ShapeDtypeStruct((1, 1), FULL), jax.ShapeDtypeStruct((4, 2) + stats.shape[2:], FULL)),
+        in_specs=[smem_spec()] + [vmem_spec()] * 2 + [any_spec()] * 2 + [vmem_spec()] * 2 + [any_spec()] * 4,
+        out_specs=(any_spec(),) * 4 + (vmem_spec(),) * 2 + (smem_spec(), any_spec()),
         scratch_shapes=[
             vm((WINDOW * TILE, 128), FULL), vm((WINDOW, TILE, 128), LOW),
             vm((FRONT + WINDOW * TILE, 128), FULL), vm((rows, 128), FULL), vm((rows, 128), FULL),
-            vm((rows, 128), FULL), vm((128, 128), FULL), sem((3, PIECES)), sem((4, PIECES)), sem((4,)),
+            vm((rows, 128), FULL), vm((128, 128), FULL), sem((3, PIECES)), sem((4, PIECES)), sem((4,)), sem((4,)),
         ],
         compiler_params=pltpu.CompilerParams(vmem_limit_bytes=60 << 20),
     )(owners, factor, norm, big.reshape(BIG_ROWS, 128), small.reshape(USED_TILES[1], TILE, 128),
       gram_old, basis_old, params.reshape(span, 1, 128), moment.reshape(span, 1, 128),
-      second.reshape(span, 1, 128))
+      second.reshape(span, 1, 128), stats)
     return tuple(out.reshape(1, span * 128) for out in outs[:4]) + outs[4:]
-
-
-def to_phases(teach, stud):
-    def split(part, axes):
-        crops, high, across, channels = part.shape
-        part = part.reshape(crops, high // 2, 2, across // 2, 2, channels).transpose(axes)
-        return part.reshape(4, -1, channels)
-
-    zeros = jnp.zeros((4, PADDED - ROWS, teach.shape[-1]), teach.dtype)
-    parts = [split(stud, (2, 4, 0, 1, 3, 5)), split(teach, (2, 4, 1, 3, 0, 5)), zeros]
-    return jnp.concatenate(parts, axis=1)
-
-
-def from_phases(phases, shape, crops_last):
-    crops, high, across, channels = shape
-    if crops_last:
-        part = phases.reshape(2, 2, high // 2, across // 2, crops, channels).transpose(4, 2, 0, 3, 1, 5)
-    else:
-        part = phases.reshape(2, 2, crops, high // 2, across // 2, channels).transpose(2, 3, 0, 4, 1, 5)
-    return part.reshape(shape)
 
 
 def on_small_slice(
@@ -2271,33 +2285,34 @@
     gram_stats,
     eigen_basis,
 ):
-    phases = to_phases(teach_in[0], stud_in[0])
+    teach_shape, stud_shape = teach_in.shape[1:], stud_in.shape[1:]
+    teach_x = teach_in[0].transpose(1, 2, 0, 3).reshape(-1, C_IN)
+    stud_x = stud_in[0].reshape(-1, C_IN)
     big, small, ids = prepare(owners, params)
     all_big, all_small, table = gather_all(big, small, ids)
-    wide_0, wide_1, final, stats, grad_x, out_big, out_small = run_step(
+    wide_0, wide_1, final, stats, teach_grad, stud_grad, out_big, out_small = run_step(
         table,
         depth_gates,
         teach_ids.T,
         stud_ids,
         all_big.reshape(2, 8, BIG_ROWS, 128),
         all_small.reshape(2, USED_TILES[1], TILE, 128),
-        phases,
+        teach_x,
+        stud_x,
         targets,
     )
     sum_big, sum_small, segment_stud, segment_teach, stats, norm, factor = reduce_all(
         out_big, out_small, wide_0, wide_1, final, stats, table
     )
-    clipped, moment_new, second_new, params_new, gram_new, rotation, length = update(
-        owners, factor, norm, sum_big, sum_small, gram_stats[0], eigen_basis[0], params, moment, second
-    )
-    teach_shape, stud_shape = teach_in.shape[1:], stud_in.shape[1:]
+    clipped, moment_new, second_new, params_new, gram_new, rotation, length, stats = update(
+        owners, factor, norm, sum_big, sum_small, gram_stats[0], eigen_basis[0], params, moment, second, stats
+    )
     small_teach = (teach_shape[1] // 2, teach_shape[2] // 2, teach_shape[0], C_OUT)
     small_stud = (stud_shape[0], stud_shape[1] // 2, stud_shape[2] // 2, C_OUT)
     segment_teach = segment_teach[:, : ROWS - STUD_ROWS].reshape((4,) + small_teach).transpose(0, 3, 1, 2, 4)
     segment_stud = segment_stud.reshape((4,) + small_stud)
-    stats = stats[:, 0:2]
-    teach_grad = from_phases(grad_x[:, STUD_ROWS:ROWS], teach_shape, True)
-    stud_grad = from_phases(grad_x[:, :STUD_ROWS], stud_shape, False)
+    teach_grad = teach_grad.reshape(teach_shape[1:3] + (teach_shape[0], C_IN)).transpose(2, 0, 1, 3)
+    stud_grad = stud_grad.reshape(stud_shape)
     grad_norm = length.reshape(())
     return (
         segment_teach[None],

time: 307 us -> 299 us (0.974)
  Pallas kernels: 291 us -> 287 us
  local copies, waits for them, and re-layouts: 11.2 us -> 7.91 us
    pallas_call x1, Pallas kernels: 109 us -> 106 us  [gather_all(): pl.pallas_call(gather_kernel, name='gather_all', out_shape=(jax.ShapeDtyp...]
where the time goes in v1:
time: 299 us; the launch traced here: 296 us
  Pallas kernels  287 us (96%)
  local copies, waits for them, and re-layouts  7.91 us (3%)
    pallas_call x1, Pallas kernels, reduce_all(): pl.pallas_call(reduce_kernel, name='reduce_all', out_shape=(jax.ShapeDtyp...  122 us
    pallas_call x1, Pallas kernels, gather_all(): pl.pallas_call(gather_kernel, name='gather_all', out_shape=(jax.ShapeDtyp...  106 us
    pallas_call x1, Pallas kernels, run_step(): pl.pallas_call(step_kernel, name='step', out_shape=(wide, wide, wide, jax...  36.2 us
    pallas_call x1, Pallas kernels, update(): pl.pallas_call(update_kernel, name='update', out_shape=(flat_shape,) * 4...  18.4 us

profile of v1, /device:TPU:0, one launch (start us, length us, event | category | flops | bytes accessed | tf_op | source)
XLA Modules:
  0.0 296.3 jit_solution(15921233034656893626)
XLA Ops:
  0.6 2.6 reshape.83.teach_x
  3.3 5.4 %prepare.1 = (bf16[4928,128]{1,0:T(8,128)(2,1)}, bf16[33,256,128]{2,1,0:T(8,128)(2,1)}, s32[8,128]{1,0:T(8,128)}) custom-call(s32[1,8]{1,0:T(1,128)} %owners.3, f32[4870,1,128]{2,1,0:T(1,128)} %bitcast.36), custom_call_target="tpu_custom_call" | custom-call | tf_op jit(solution)/shard_map/prepare/pallas_call | solution.py:570
  8.7 105.7 %gather_all.1 = (bf16[2,8,2,2464,128]{4,3,2,1,0:T(8,128)(2,1)}, bf16[2,8,2,528,128]{4,3,2,1,0:T(8,128)(2,1)}, s32[4,8,128]{2,1,0:T(8,128)}) custom-call(bf16[4928,128]{1,0:T(8,128)(2,1)} %get-tuple-element.41.big, bf16[8,1056,128]{2,1,0:T(8,128)(2,1)} %bitcast.44, s32[8,128]{1,0:T(8,128)} %get-tuple-element.43.ids), custom_call_target="tpu_custom_call" | custom-call | tf_op jit(solution)/shard_map/gather_all/pallas_call | solution.py:990
  114.3 36.2 %step.1 = (bf16[128,2048]{1,0:T(8,128)(2,1)}, bf16[128,2048]{1,0:T(8,128)(2,1)}, bf16[128,2048]{1,0:T(8,128)(2,1)}, f32[4,8,3072]{2,1,0:T(8,128)}, bf16[288,1024...) custom-call(s32[4,8,128]{2,1,0:T(8,128)} %get-tuple-element.44.table, ...), custom_call_target="tpu_custom_call" | custom-call | tf_op jit(solution)/shard_map/step/pallas_call | solution.py:1515
  150.6 121.9 %reduce_all.1 = (f32[2,2464,128]{2,1,0:T(8,128)}, bf16[8,1056,128]{2,1,0:T(8,128)(2,1)}, bf16[4,48,2048]{2,1,0:T(8,128)(2,1)}, bf16[4,80,2048]{2,1,0:T(8,128)(2,...) custom-call(bf16[2,8,2,2464,128]{4,3,2,1,0:T(8,128)(2,1)} %bitcast.34, ...), custom_call_target="tpu_custom_call" | custom-call | tf_op jit(solution)/shard_map/reduce_all/pallas_call | solution.py:2049
  272.4 0.0 copy-start.1
  272.5 0.0 copy-start
  272.5 1.5 slice.3
  273.9 1.6 reshape.86
  275.5 0.0 copy-done.1
  275.5 1.0 reshape.87
  276.6 0.0 copy-done
  276.6 1.2 broadcast_in_dim_reshape.6
  277.7 18.4 %update.1 = (f32[4870,1,128]{2,1,0:T(1,128)}, f32[4870,1,128]{2,1,0:T(1,128)}, f32[4870,1,128]{2,1,0:T(1,128)}, f32[4870,1,128]{2,1,0:T(1,128)}, f32[128,128]{1,...) custom-call(s32[1,8]{1,0:T(1,128)} %owners.3, f32[8,128]{1,0:T(8,128)} %get-tuple-element.57.factor_ref, ...), custom_call_target="tpu_custom_call" | custom-call | tf_op jit(solution)/shard_map/update/pallas_call | solution.py:2256
Async XLA Ops:
  272.4 3.1 %copy-start.1 = (bf16[288,1024]{1,0:T(8,128)(2,1)S(1)}, bf16[288,1024]{1,0:T(8,128)(2,1)}, u32[]{:S(2)}) copy-start(bf16[288,1024]{1,0:T(8,128)(2,1)} %get-tuple-element.55) | copy-start | bytes 1769476
  272.5 4.1 %copy-start = (bf16[4,48,2048]{2,1,0:T(8,128)(2,1)S(1)}, bf16[4,48,2048]{2,1,0:T(8,128)(2,1)}, u32[]{:S(2)}) copy-start(bf16[4,48,2048]{2,1,0:T(8,128)(2,1)} %get-tuple-element.54) | copy-start | bytes 2359300
